TPU v7x, 32 devices: a whole 2x2x4 slice. The times are simulated.
32 devices in a mesh: seq: 8 (over z, y), mp: 4 (over x, core).
Axes of the slice: x: 2, y: 2, z: 4, core: 2. Of those that a mesh axis runs over, the one named last changes fastest.
Arguments:
- queries: bfloat16 [4096, 8192], P('seq', 'mp'), may hold values from -6 to 6
- keys_in: bfloat16 [4096, 8192], P('seq', 'mp'), may hold values from -6 to 6
- values_in: bfloat16 [4096, 8192], P('seq', 'mp'), may hold values from -6 to 6
- residual: bfloat16 [4096, 8192], P('seq', 'mp')
- short_taps: bfloat16 [3, 7, 8192], P(None, None, 'mp'), may hold values from -2 to 2
- mr_filter: bfloat16 [128, 512], P('seq', 'mp'), may hold values from -0.5 to 0.5
- norm_gain: bfloat16 [8192], P('mp'), may hold values from 0.5 to 1.5
- predecessor: int32 [8], replicated, may hold values from -1 to 7, as said below
- stretch_lengths: int32 [8], replicated, may hold values from 1 to 512, as said below
Outputs:
- mixed: bfloat16 [4096, 8192], P('seq', 'mp')
- normed: bfloat16 [4096, 8192], P('seq', 'mp')
Inputs may be any that keep to these rules, and one draw needn't show every extreme that they name: predecessor[j] is the stretch holding the preceding 512 tokens of stretch j's genome, or -1 for a genome's first stretch; each stretch precedes at most one stretch, and the chains have no cycles. `stretch_lengths`: every stretch that precedes another stretch is full (512 valid tokens); valid tokens come first.
All inputs are finite; a program needn't handle non-finite values.
Results may differ from a plain program's by a relative error of at most 0.0049.
Values may be sent and summed in bfloat16 or wider, within the bound.
No kernel may reach another device: no remote copies, remote signals or barrier semaphores. Data moves between devices by JAX's collectives and lax.ppermute only.
A program may use at most 64 MiB of HBM per device.

v0:
```python
import functools

import jax
import jax.numpy as jnp
from jax import lax
from jax.experimental import pallas as pl
from jax.experimental.pallas import tpu as pltpu
from jax.sharding import PartitionSpec as P

EPSILON = 1e-06
F32 = jnp.float32
BF16 = jnp.bfloat16
LANES = 128
STEP = 256
WIDE = 512
SIDE = 4
BLOCK = 32
WINDOW = 256
PACKED = 160
OPENING = 144
VMEM_LIMIT = 64 * 1024 * 1024


def unfold(picked):
    return jnp.concatenate([picked[:, i * LANES : (i + 1) * LANES] for i in range(picked.shape[1] // LANES)])


def params():
    return pltpu.CompilerParams(vmem_limit_bytes=VMEM_LIMIT)


def cost(flops, bytes_accessed):
    return pl.CostEstimate(flops=flops, bytes_accessed=bytes_accessed, transcendentals=0)


def short_conv(scratch, taps, start, rows):
    total = None
    for offset in range(taps.shape[0]):
        term = taps[offset : offset + 1] * scratch[pl.ds(start + 8 - offset, rows), :]
        total = term if total is None else total + term
    return total


def tail_kernel(packed, q_ref, k_ref, v_ref, kb_ref, vb_ref, taps_ref, filt_ref, out_ref, ks, vs):
    for slot in range(out_ref.shape[0]):
        lasts = []
        for tile in range(STEP // LANES):
            number = slot * (STEP // LANES) + tile
            cols = slice(number * LANES, (number + 1) * LANES)
            here = slice(tile * LANES, (tile + 1) * LANES)
            kt, vt = ks.at[number], vs.at[number]
            kt[0:16, :] = kb_ref[:, cols].astype(F32)
            vt[0:16, :] = vb_ref[:, cols].astype(F32)
            kt[16:144, :] = k_ref[:, cols].astype(F32)
            vt[16:144, :] = v_ref[:, cols].astype(F32)
            key_taps = taps_ref[1, :, cols].astype(F32)
            value_taps = taps_ref[2, :, cols].astype(F32)
            for row in range(0, 128, 64):
                key = short_conv(kt, key_taps, row + 8, 64)
                value = short_conv(vt, value_taps, row + 8, 64)
                out_ref[slot, row : row + 64, here] = (key * value).astype(BF16)
            last = [q_ref[:, cols].astype(F32)[8:], kt[136:144, :], vt[136:144, :]]
            if packed:
                last.append(filt_ref[...].astype(F32)[8 * tile : 8 * tile + 8])
            else:
                last.append(jnp.zeros((8, LANES), F32))
            lasts.append(jnp.concatenate(last))
        out_ref[slot, 128:PACKED, :] = jnp.concatenate(lasts, axis=1).astype(BF16)


def tail_call(packed, queries, keys_in, values_in, short_taps, mr_filter):
    rows, width = queries.shape
    slots = width // STEP
    part = width // 2
    count = part // LANES
    return pl.pallas_call(
        functools.partial(tail_kernel, packed),
        grid=(2,),
        in_specs=[
            pl.BlockSpec((16, part), lambda p: (rows // 16 - 1, p)),
            pl.BlockSpec((128, part), lambda p: (rows // 128 - 1, p)),
            pl.BlockSpec((128, part), lambda p: (rows // 128 - 1, p)),
            pl.BlockSpec((16, part), lambda p: (rows // 16 - 9, p)),
            pl.BlockSpec((16, part), lambda p: (rows // 16 - 9, p)),
            pl.BlockSpec((3, 7, part), lambda p: (0, 0, p)),
            pl.BlockSpec(mr_filter.shape, lambda p: (0, 0)),
        ],
        out_specs=pl.BlockSpec((slots // 2, PACKED, STEP), lambda p: (p, 0, 0)),
        out_shape=jax.ShapeDtypeStruct((slots, PACKED, STEP), BF16),
        scratch_shapes=[pltpu.VMEM((count, 144, LANES), F32)] * 2,
        compiler_params=params(),
        cost_estimate=cost(128 * width * 30, 128 * width * 6),
        name="tail",
    )(queries, keys_in, values_in, keys_in, values_in, short_taps, mr_filter)


def feature_kernel(q_ref, k_ref, v_ref, taps_ref, out_ref, opening_ref, later_ref, qs, ks, vs):
    rows = k_ref.shape[0]

    def pair(index, carry):
        for tile in range(2):
            cols = pl.ds(pl.multiple_of(index * 2 * LANES + tile * LANES, LANES), LANES)
            scratches = (qs.at[tile], ks.at[tile], vs.at[tile])
            taps = [taps_ref[i, :, cols].astype(F32) for i in range(3)]
            for scratch, ref in zip(scratches, (q_ref, k_ref, v_ref)):
                scratch[0:8, :] = jnp.zeros((8, LANES), F32)
                scratch[8 : rows + 8, :] = ref[:, cols].astype(F32)
            for row in range(0, rows, 64):
                query, key, value = [short_conv(x, t, row, 64) for x, t in zip(scratches, taps)]
                out_ref[row : row + 64, cols] = (key * value).astype(BF16)
                if row < OPENING:
                    count = min(64, OPENING - row)
                    opening_ref[row : row + count, cols] = query[:count]
                if row >= 128:
                    later_ref[row - 128 : row - 64, cols] = query
        return carry

    lax.fori_loop(0, k_ref.shape[1] // (2 * LANES), pair, 0)


def feature_call(queries, keys_in, values_in, short_taps):
    rows, width = keys_in.shape
    heights = (rows, OPENING, rows - 128)
    blocks = [pl.BlockSpec((height, WIDE), lambda p: (0, p)) for height in heights]
    scratch = pltpu.VMEM((2, rows + 8, LANES), F32)
    return pl.pallas_call(
        feature_kernel,
        grid=(width // WIDE,),
        in_specs=[blocks[0]] * 3 + [pl.BlockSpec((3, 7, WIDE), lambda p: (0, 0, p))],
        out_specs=blocks,
        out_shape=[
            jax.ShapeDtypeStruct((height, width), kind) for height, kind in zip(heights, (BF16, F32, F32))
        ],
        scratch_shapes=[scratch] * 3,
        compiler_params=params(),
        cost_estimate=cost(rows * width * 45, rows * width * 13),
        name="features",
    )(queries, keys_in, values_in, short_taps)


def route_kernel(pred_ref, in_ref, out_ref):
    for j in range(in_ref.shape[0]):
        out_ref[j] = in_ref[jnp.maximum(pred_ref[j], 0)]


def route_call(predecessor, received):
    return pl.pallas_call(
        route_kernel,
        in_specs=[pl.BlockSpec(memory_space=pltpu.SMEM), pl.BlockSpec(memory_space=pltpu.VMEM)],
        out_specs=pl.BlockSpec(memory_space=pltpu.VMEM),
        out_shape=jax.ShapeDtypeStruct(received.shape, BF16),
        compiler_params=params(),
        cost_estimate=cost(0, received.size * 4),
        name="route",
    )(predecessor, received)


def all_taps(filt_ref):
    if len(filt_ref.shape) == 2:
        return filt_ref[...]
    rows = []
    for j in range(filt_ref.shape[0]):
        last = filt_ref[j].astype(F32)[8:]
        rows += [last[:, :LANES], last[:, LANES:]]
    return jnp.concatenate(rows).astype(BF16)


def spread_taps(filter_rows):
    shape = (filter_rows.shape[0], WINDOW)
    tap = lax.broadcasted_iota(jnp.int32, shape, 0)
    place = lax.broadcasted_iota(jnp.int32, shape, 1)
    onehot = (place == WINDOW - BLOCK - tap).astype(BF16)
    return lax.dot_general(filter_rows, onehot, (((0,), (0,)), ((), ())), preferred_element_type=F32)


def toeplitz(lines):
    blocks = []
    for g in range(lines.shape[0]):
        line = jnp.broadcast_to(lines[g : g + 1], (BLOCK, WINDOW))
        blocks.append(pltpu.roll(line, 0, 1, stride=1, stride_axis=0).astype(BF16))
    return jnp.concatenate(blocks)


def pick_groups(result, group_size, rows=BLOCK):
    shape = (rows, result.shape[1])
    group = (lax.broadcasted_iota(jnp.int32, shape, 1) & (LANES - 1)) // group_size
    picked = result[:rows]
    for g in range(1, LANES // group_size):
        picked = jnp.where(group == g, result[g * rows : (g + 1) * rows], picked)
    return picked


def main_kernel(group_size, len_ref, query_ref, u_ref, res_ref, filt_ref, mixed_ref, sum_ref, lines_ref, acc):
    step = pl.program_id(0)
    rows = u_ref.shape[0]
    per_lane = LANES // group_size
    length = len_ref[lax.axis_index("seq")]

    @pl.when(step == 0)
    def _():
        lines_ref[...] = spread_taps(all_taps(filt_ref))
        acc[...] = jnp.zeros_like(acc)

    def tiles():
        for number in range(WIDE // LANES):
            cols = slice(number * LANES, (number + 1) * LANES)
            base = pl.multiple_of((step * (WIDE // LANES) + number) * per_lane, per_lane)
            matrix = toeplitz(lines_ref[pl.ds(base, per_lane), :])
            for start in range(128, rows, SIDE * BLOCK):
                windows = []
                for first in range(start, start + SIDE * BLOCK, BLOCK):
                    low = first + BLOCK - WINDOW
                    if low < 0:
                        windows.append(
                            jnp.concatenate([jnp.zeros((-low, LANES), BF16), u_ref[0 : first + BLOCK, cols]])
                        )
                    else:
                        windows.append(u_ref[low : first + BLOCK, cols])
                result = jnp.dot(matrix, jnp.concatenate(windows, axis=1), preferred_element_type=F32)
                picked = pick_groups(result, group_size)
                filtered = unfold(picked)
                here = slice(start - 128, start - 128 + SIDE * BLOCK)
                row = lax.broadcasted_iota(jnp.int32, filtered.shape, 0) + start
                mixed = jnp.where(row < length, query_ref[here, cols] * filtered, 0.0).astype(BF16)
                mixed_ref[here, cols] = mixed
                summed = res_ref[here, cols].astype(F32) + mixed.astype(F32)
                acc[here, :] += summed * summed

    tiles()

    @pl.when(step == pl.num_programs(0) - 1)
    def _():
        sum_ref[...] = jnp.sum(acc[...].T, axis=0, keepdims=True)


def main_call(group_size, stretch_lengths, query_later, mixed_in, residual, filter_rows):
    rows, width = residual.shape
    groups = width // group_size
    if len(filter_rows.shape) == 2:
        filter_spec = pl.BlockSpec(filter_rows.shape, lambda p, *_: (0, 0))
    else:
        filter_spec = pl.BlockSpec((filter_rows.shape[0], 16, STEP), lambda p, *_: (0, PACKED // 16 - 1, 0))
    block = pl.BlockSpec((rows, WIDE), lambda p, *_: (0, p))
    later = pl.BlockSpec((pl.Element(rows - 128), pl.Element(WIDE)), lambda p, *_: (128, p * WIDE))
    return pl.pallas_call(
        functools.partial(main_kernel, group_size),
        grid_spec=pltpu.PrefetchScalarGridSpec(
            num_scalar_prefetch=1,
            grid=(width // WIDE,),
            in_specs=[
                pl.BlockSpec((rows - 128, WIDE), lambda p, *_: (0, p)),
                block,
                later,
                filter_spec,
            ],
            out_specs=[
                later,
                pl.BlockSpec((1, rows - 128), lambda p, *_: (0, 0)),
                pl.BlockSpec((groups, WINDOW), lambda p, *_: (0, 0)),
            ],
            scratch_shapes=[
                pltpu.VMEM((rows - 128, LANES), F32),
            ],
        ),
        out_shape=[
            jax.ShapeDtypeStruct((rows, width), BF16),
            jax.ShapeDtypeStruct((1, rows - 128), F32),
            jax.ShapeDtypeStruct((groups, WINDOW), F32),
        ],
        compiler_params=params(),
        cost_estimate=cost(rows * width * 2 * WINDOW * 8, rows * width * 12),
        name="conv",
    )(stretch_lengths, query_later, mixed_in, residual, filter_rows)


def head_kernel(group_size, pred_ref, len_ref, held, query_ref, q_ref, k_ref, v_ref, u_ref, res_ref, taps_ref, lines_ref, kept_ref, mixed_ref, sum_ref, qs, ks, vs, acc):
    del kept_ref
    step = pl.program_id(0)
    per_lane = LANES // group_size
    device = lax.axis_index("seq")
    length = len_ref[device]
    follows = pred_ref[device] >= 0

    @pl.when(step == 0)
    def _():
        acc[...] = jnp.zeros_like(acc)

    def tiles():
        for number in range(WIDE // LANES):
            index, tile = divmod(number, STEP // LANES)
            cols = slice(number * LANES, (number + 1) * LANES)
            here = slice(tile * LANES, (tile + 1) * LANES)
            qt, kt, vt = qs.at[number], ks.at[number], vs.at[number]
            prev = jnp.where(follows, held[index, 128:PACKED, here].astype(F32), 0.0)
            qt[0:8, :] = prev[0:8]
            kt[0:8, :] = prev[8:16]
            vt[0:8, :] = prev[16:24]
            qt[8:24, :] = q_ref[:, cols].astype(F32)
            kt[8:24, :] = k_ref[:, cols].astype(F32)
            vt[8:24, :] = v_ref[:, cols].astype(F32)
            first_query = short_conv(qt, taps_ref[0, :, cols].astype(F32), 0, 16)
            key = short_conv(kt, taps_ref[1, :, cols].astype(F32), 0, 16)
            value = short_conv(vt, taps_ref[2, :, cols].astype(F32), 0, 16)
            opening = (key * value).astype(BF16)
            state = held[index, 0:128, here]
            state = jnp.where(follows, state, jnp.zeros_like(state))
            pad = jnp.zeros((WINDOW - BLOCK - 128, LANES), BF16)
            extended = jnp.concatenate([pad, state, opening, u_ref[16:192, cols]])
            base = number * per_lane
            matrix = toeplitz(lines_ref[pl.ds(base, per_lane), :])
            parts = []
            for first in range(0, 128, SIDE * BLOCK):
                lows = range(first, first + SIDE * BLOCK, BLOCK)
                windows = [extended[low : low + WINDOW] for low in lows]
                result = jnp.dot(matrix, jnp.concatenate(windows, axis=1), preferred_element_type=F32)
                picked = pick_groups(result, group_size)
                parts.append((first, SIDE * BLOCK, unfold(picked)))
            edge = OPENING - 128
            edge_matrix = jnp.concatenate([matrix[g * BLOCK : g * BLOCK + edge] for g in range(per_lane)])
            edge_result = jnp.dot(edge_matrix, extended[128 : 128 + WINDOW], preferred_element_type=F32)
            parts.append((128, edge, pick_groups(edge_result, group_size, edge)))
            for first, rows, filtered in parts:
                query = query_ref[first : first + rows, cols]
                if first == 0:
                    query = jnp.concatenate([first_query, query[16:]])
                row = lax.broadcasted_iota(jnp.int32, (rows, LANES), 0) + first
                mixed = jnp.where(row < length, query * filtered, 0.0).astype(BF16)
                mixed_ref[first : first + rows, cols] = mixed
                summed = res_ref[first : first + rows, cols].astype(F32) + mixed.astype(F32)
                acc[first : first + rows, :] += summed * summed

    tiles()

    @pl.when(step == pl.num_programs(0) - 1)
    def _():
        sum_ref[...] = jnp.sum(acc[...].T, axis=0, keepdims=True)


def head_call(group_size, predecessor, stretch_lengths, previous, query_opening, queries, keys_in, values_in, mixed_in, residual, short_taps, lines, mixed):
    rows, width = queries.shape
    per_step = WIDE // group_size
    block = pl.BlockSpec((OPENING, WIDE), lambda p, *_: (0, p))
    small = pl.BlockSpec((16, WIDE), lambda p, *_: (0, p))
    return pl.pallas_call(
        functools.partial(head_kernel, group_size),
        grid_spec=pltpu.PrefetchScalarGridSpec(
            num_scalar_prefetch=2,
            grid=(width // WIDE,),
            in_specs=[
                pl.BlockSpec((WIDE // STEP, PACKED, STEP), lambda p, *_: (p, 0, 0)),
                block,
                small,
                small,
                small,
                pl.BlockSpec((192, WIDE), lambda p, *_: (0, p)),
                block,
                pl.BlockSpec((3, 7, WIDE), lambda p, *_: (0, 0, p)),
                pl.BlockSpec((per_step, WINDOW), lambda p, *_: (p, 0)),
                pl.BlockSpec(memory_space=pl.ANY),
            ],
            out_specs=[block, pl.BlockSpec((1, 256), lambda p, *_: (0, 0))],
            scratch_shapes=[
                pltpu.VMEM((WIDE // LANES, 24, LANES), F32),
                pltpu.VMEM((WIDE // LANES, 24, LANES), F32),
                pltpu.VMEM((WIDE // LANES, 24, LANES), F32),
                pltpu.VMEM((256, LANES), F32),
            ],
        ),
        out_shape=[
            jax.ShapeDtypeStruct((rows, width), BF16),
            jax.ShapeDtypeStruct((1, 256), F32),
        ],
        input_output_aliases={11: 0},
        compiler_params=params(),
        cost_estimate=cost(128 * width * 2 * WINDOW * 8, 128 * width * 12),
        name="head",
    )(predecessor, stretch_lengths, previous, query_opening, queries, keys_in, values_in, mixed_in, residual, short_taps, lines, mixed)


def norm_kernel(channels, first_block, sums, len_ref, *refs):
    sum_refs, (mixed_ref, res_ref, gain_ref), out_ref = refs[:sums], refs[sums : sums + 3], refs[-1]
    rows = mixed_ref.shape[0]
    first = (pl.program_id(0) + first_block) * rows
    length = len_ref[lax.axis_index("seq")]
    total = sum_refs[0][...]
    for ref in sum_refs[1:]:
        total = total + ref[...]
    scale = jnp.broadcast_to(lax.rsqrt(total / channels + EPSILON), (LANES, total.shape[1])).T[:rows]
    scale = jnp.where(lax.broadcasted_iota(jnp.int32, (rows, LANES), 0) + first < length, scale, 0.0)
    for lane in range(0, mixed_ref.shape[1], LANES):
        cols = slice(lane, lane + LANES)
        gain = gain_ref[:, cols].astype(F32)
        summed = res_ref[:, cols].astype(F32) + mixed_ref[:, cols].astype(F32)
        out_ref[:, cols] = (summed * scale * gain).astype(BF16)


def norm_call(channels, steps, first_block, stretch_lengths, totals, mixed, residual, gain, normed=None):
    rows, width = mixed.shape
    opening = first_block == 0
    size, lanes, skip = (OPENING, 256, 0) if opening else (128, 128, first_block - 1)
    block = pl.BlockSpec((size, width), lambda p, *_: (p + first_block, 0))
    operands = [*totals, mixed, residual, gain]
    in_specs = [pl.BlockSpec((1, lanes), lambda p, *_: (0, p + skip))] * len(totals)
    in_specs += [block, block, pl.BlockSpec((1, width), lambda p, *_: (0, 0))]
    aliases = {}
    if normed is not None:
        aliases = {len(operands) + 1: 0}
        operands.append(normed)
        in_specs.append(pl.BlockSpec(memory_space=pl.ANY))
    return pl.pallas_call(
        functools.partial(norm_kernel, channels, first_block, len(totals)),
        grid_spec=pltpu.PrefetchScalarGridSpec(
            num_scalar_prefetch=1, grid=(steps,), in_specs=in_specs, out_specs=block
        ),
        out_shape=jax.ShapeDtypeStruct((rows, width), BF16),
        input_output_aliases=aliases,
        compiler_params=params(),
        cost_estimate=cost(steps * size * width * 6, steps * size * width * 6),
        name="norm%d" % first_block,
    )(stretch_lengths, *operands)


def swap(array, axis, distance):
    size = lax.axis_size(axis)
    return lax.ppermute(array, axis, [(i, i ^ distance) for i in range(size)])


def exchange(pieces):
    return lax.all_to_all(pieces, "seq", split_axis=0, concat_axis=0, tiled=True)


def shares(squares):
    parts = lax.axis_size("mp")
    if parts != 4:
        return [lax.psum(squares, "mp")]
    return [squares] + [swap(squares, "mp", k) for k in range(1, parts)]


def body(queries, keys_in, values_in, residual, short_taps, mr_filter, norm_gain, predecessor, stretch_lengths):
    rows, width = queries.shape
    count = lax.axis_size("seq")
    channels = width * lax.axis_size("mp")
    group_size = width // mr_filter.shape[1]
    two_phase = width // STEP == count == 8 and mr_filter.shape == (16, LANES)
    gain = norm_gain.reshape(1, width)
    packed = tail_call(two_phase, queries, keys_in, values_in, short_taps, mr_filter)
    mixed_in, query_opening, query_later = feature_call(queries, keys_in, values_in, short_taps)
    if two_phase:
        received = exchange(packed)
        received, mixed_in, gain = lax.optimization_barrier((received, mixed_in, gain))
        routed, filter_rows = lax.optimization_barrier((route_call(predecessor, received), received))
        previous = exchange(routed)
    else:
        gathered = lax.all_gather(packed[None], "seq", axis=0, tiled=True)
        source = jnp.clip(predecessor[lax.axis_index("seq")], 0, count - 1)
        previous = lax.dynamic_index_in_dim(gathered, source, 0, keepdims=False)
        filter_rows = lax.all_gather(mr_filter, "seq", axis=0, tiled=True)
    mixed, squares, lines = main_call(
        group_size, stretch_lengths, query_later, mixed_in, residual, filter_rows
    )
    totals = shares(squares)
    early = rows // 128 - 2
    normed = norm_call(channels, early, 1, stretch_lengths, totals, mixed, residual, gain)
    previous, normed = lax.optimization_barrier((previous, normed))
    mixed, squares = head_call(
        group_size, predecessor, stretch_lengths, previous, query_opening, queries, keys_in, values_in,
        mixed_in, residual, short_taps, lines, mixed,
    )
    opening_totals = shares(squares)
    normed = norm_call(channels, 1, early + 1, stretch_lengths, totals, mixed, residual, gain, normed)
    normed = norm_call(channels, 1, 0, stretch_lengths, opening_totals, mixed, residual, gain, normed)
    return (mixed, normed)


def solution(mesh):
    in_specs = (
        P("seq", "mp"),
        P("seq", "mp"),
        P("seq", "mp"),
        P("seq", "mp"),
        P(None, None, "mp"),
        P("seq", "mp"),
        P("mp"),
        P(),
        P(),
    )
    out_specs = (P("seq", "mp"), P("seq", "mp"))
    return jax.shard_map(body, mesh=mesh, in_specs=in_specs, out_specs=out_specs, check_vma=False)
```

profile of v0, /device:TPU:0, one launch (start us, length us, event | category | flops | bytes accessed | tf_op | source)
XLA Modules:
  0.0 65.5 jit_solution(4926558730985064809)
XLA Ops:
  0.6 3.1 %tail.1 = bf16[8,160,256]{2,1,0:T(8,128)(2,1)} custom-call(bf16[512,2048]{1,0:T(8,128)(2,1)} %q_ref.5, bf16[512,2048]{1,0:T(8,128)(2,1)} %k_ref.5, bf16[512,2048]{1,0:T(8,128)(2,1)} %v_ref.5, bf16[512,2048]{1,0:T(8,128)(2,1)} %k_ref.5, bf16[512,2048]{1,0:T(8,128)(2,1)} %v_ref.5, bf16[3,7,2048]{2,1,0:T(8,128)(2,1)} %taps_ref.5, bf16[16,128]{1,0:T(8,128)(2,1)} %filt_ref.1), custom_call_target="tpu_custom_call" | custom-call | flops 7864320 | bytes 1572864 | tf_op jit(solution)/shard_map/tail/pallas_call | solution.py:76
  3.7 7.3 %all-to-all-start = ((bf16[8,160,256]{2,1,0:T(8,128)(2,1)}), bf16[8,160,256]{2,1,0:T(8,128)(2,1)}, u32[]{:S(2)}, u32[]{:S(2)}) async-start(bf16[8,160,256]{2,1,0:T(8,128)(2,1)} %tail.1), calls=%async_computation | async-start | bytes 1310720 | tf_op jit(solution)/shard_map/all_to_all | solution.py:429
  11.0 1.3 %reshape.7.refs_6_ = bf16[1,2048]{1,0:T(2,128)(2,1)} reshape(bf16[2048]{0:T(1024)(128)(2,1)} %param.15) | data formatting | bytes 8192 | tf_op jit(solution)/shard_map/reshape | solution.py:445
  12.3 9.7 %features.1 = (bf16[512,2048]{1,0:T(8,128)(2,1)}, f32[144,2048]{1,0:T(8,128)}, f32[384,2048]{1,0:T(8,128)}) custom-call(bf16[512,2048]{1,0:T(8,128)(2,1)} %q_ref.5, bf16[512,2048]{1,0:T(8,128)(2,1)} %k_ref.5, bf16[512,2048]{1,0:T(8,128)(2,1)} %v_ref.5, bf16[3,7,2048]{2,1,0:T(8,128)(2,1)} %taps_ref.5), custom_call_target="tpu_custom_call" | custom-call | flops 47185920 | bytes 13631488 | tf_op jit(solution)/shard_map/features/pallas_call | solution.py:126
  22.0 6.4 %all-to-all-done.in_ref.filt_ref = bf16[8,160,256]{2,1,0:T(8,128)(2,1)} async-done(((bf16[8,160,256]{2,1,0:T(8,128)(2,1)}), bf16[8,160,256]{2,1,0:T(8,128)(2,1)}, u32[]{:S(2)}, u32[]{:S(2)}) %all-to-all-start) | async-done | bytes 655392 | tf_op jit(solution)/shard_map/all_to_all | solution.py:429
  28.4 2.0 %route.1 = bf16[8,160,256]{2,1,0:T(8,128)(2,1)} custom-call(s32[8]{0:T(128)} %pred_ref.3, bf16[8,160,256]{2,1,0:T(8,128)(2,1)} %all-to-all-done.in_ref.filt_ref), custom_call_target="tpu_custom_call" | custom-call | bytes 1310720 | tf_op jit(solution)/shard_map/route/pallas_call | solution.py:147
  30.5 4.2 %all-to-all-start.1 = ((bf16[8,160,256]{2,1,0:T(8,128)(2,1)}), bf16[8,160,256]{2,1,0:T(8,128)(2,1)}, u32[]{:S(2)}, u32[]{:S(2)}) async-start(bf16[8,160,256]{2,1,0:T(8,128)(2,1)} %route.1), calls=%async_computation.1 | async-start | bytes 1310720 | tf_op jit(solution)/shard_map/all_to_all | solution.py:429
  34.7 8.2 %conv.1 = (bf16[512,2048]{1,0:T(8,128)(2,1)}, f32[1,384]{1,0:T(1,128)}, f32[128,256]{1,0:T(8,128)}) custom-call(s32[8]{0:T(128)} %len_ref.9, f32[384,2048]{1,0:T(8,128)} %get-tuple-element.20.query_ref, bf16[512,2048]{1,0:T(8,128)(2,1)} %get-tuple-element.21.u_ref, bf16[512,2048]{1,0:T(8,128)(2,1)} %refs_5_.5, bf16[8,160,256]{2,1,0:T(8,128)(2,1)} %all-to-all-done.in_ref.filt_ref), custom_call_target="tpu_custom_call" | custom-call | flops 4294967296 | bytes 12582912 | tf_op jit(solution)/shard_map/conv/pallas_call | solution.py:245
  42.8 0.3 collective-permute-start.2
  43.1 1.3 %collective-permute-start.1 = (f32[1,384]{1,0:T(1,128)}, f32[1,384]{1,0:T(1,128)}, u32[]{:S(2)}, u32[]{:S(2)}) collective-permute-start(f32[1,384]{1,0:T(1,128)} %get-tuple-element.23.refs_0_), channel_id=1, source_target_pairs={{0,2},{1,3},{2,0},{3,1},{4,6},{5,7},{6,4},{7,5},{8,10},{9,11},{10,... | collective-permute-start | bytes 4616 | tf_op jit(solution)/shard_map/ppermute | solution.py:425
  44.4 0.3 collective-permute-start
  44.7 1.5 %collective-permute-done.2.refs_3_ = f32[1,384]{1,0:T(1,128)} collective-permute-done((f32[1,384]{1,0:T(1,128)}, f32[1,384]{1,0:T(1,128)}, u32[]{:S(2)}, u32[]{:S(2)}) %collective-permute-start.2) | collective-permute-done | bytes 1568 | tf_op jit(solution)/shard_map/ppermute | solution.py:425
  46.1 0.7 %collective-permute-done.1.refs_2_ = f32[1,384]{1,0:T(1,128)} collective-permute-done((f32[1,384]{1,0:T(1,128)}, f32[1,384]{1,0:T(1,128)}, u32[]{:S(2)}, u32[]{:S(2)}) %collective-permute-start.1) | collective-permute-done | bytes 1568 | tf_op jit(solution)/shard_map/ppermute | solution.py:425
  46.8 0.0 collective-permute-done.refs_1_
  46.8 3.3 %norm1.1.refs_7_ = bf16[512,2048]{1,0:T(8,128)(2,1)} custom-call(s32[8]{0:T(128)} %len_ref.9, f32[1,384]{1,0:T(1,128)} %get-tuple-element.23.refs_0_, f32[1,384]{1,0:T(1,128)} %collective-permute-done.refs_1_, f32[1,384]{1,0:T(1,128)} %collective-permute-done.1.refs_2_, f32[1,384]{1,0:T(1,128)} %collective-permute-done.2.refs_3_, ...), custom_call_target="tpu_custom_call" | custom-call | flops 3145728 | bytes 3145728 | tf_op jit(solution)/shard_map/norm1/pallas_call | solution.py:410
  50.2 1.5 %all-to-all-done.1.held = bf16[8,160,256]{2,1,0:T(8,128)(2,1)} async-done(((bf16[8,160,256]{2,1,0:T(8,128)(2,1)}), bf16[8,160,256]{2,1,0:T(8,128)(2,1)}, u32[]{:S(2)}, u32[]{:S(2)}) %all-to-all-start.1) | async-done | bytes 655392 | tf_op jit(solution)/shard_map/all_to_all | solution.py:429
  51.7 5.9 %head.1 = (bf16[512,2048]{1,0:T(8,128)(2,1)}, f32[1,256]{1,0:T(1,128)}) custom-call(s32[8]{0:T(128)} %pred_ref.3, s32[8]{0:T(128)} %len_ref.9, bf16[8,160,256]{2,1,0:T(8,128)(2,1)} %all-to-all-done.1.held, f32[144,2048]{1,0:T(8,128)} %get-tuple-element.27.query_ref, bf16[512,2048]{1,0:T(8,128)(2,1)} %q_ref.5, ...), custom_call_target="tpu_custom_call", output_to_operand_aliasing={{0}: (11, {})} | custom-call | flops 1073741824 | bytes 3145728 | tf_op jit(solution)/shard_map/head/pallas_call | solution.py:344
  57.6 0.1 collective-permute-start.5
  57.6 1.6 %collective-permute-start.4 = (f32[1,256]{1,0:T(1,128)}, f32[1,256]{1,0:T(1,128)}, u32[]{:S(2)}, u32[]{:S(2)}) collective-permute-start(f32[1,256]{1,0:T(1,128)} %get-tuple-element.30.refs_0_), channel_id=1, source_target_pairs={{0,2},{1,3},{2,0},{3,1},{4,6},{5,7},{6,4},{7,5},{8,10},{9,11},{10,... | collective-permute-start | bytes 3080 | tf_op jit(solution)/shard_map/ppermute | solution.py:425
  59.2 0.3 collective-permute-start.3
  59.5 3.0 %norm3.1.refs_7_ = bf16[512,2048]{1,0:T(8,128)(2,1)} custom-call(s32[8]{0:T(128)} %len_ref.9, f32[1,384]{1,0:T(1,128)} %get-tuple-element.23.refs_0_, f32[1,384]{1,0:T(1,128)} %collective-permute-done.refs_1_, f32[1,384]{1,0:T(1,128)} %collective-permute-done.1.refs_2_, f32[1,384]{1,0:T(1,128)} %collective-permute-done.2.refs_3_, ...), custom_call_target="tpu_custom_call", output_to_operand_aliasing={{}: (8, {})} | custom-call | flops 1572864 | bytes 1572864 | tf_op jit(solution)/shard_map/norm3/pallas_call | solution.py:410
  62.4 0.0 collective-permute-done.5.refs_3_
  62.4 0.0 collective-permute-done.4.refs_2_
  62.5 3.0 %norm0.1 = bf16[512,2048]{1,0:T(8,128)(2,1)} custom-call(s32[8]{0:T(128)} %len_ref.9, f32[1,256]{1,0:T(1,128)} %get-tuple-element.30.refs_0_, f32[1,256]{1,0:T(1,128)} %collective-permute-done.3.refs_1_, f32[1,256]{1,0:T(1,128)} %collective-permute-done.4.refs_2_, f32[1,256]{1,0:T(1,128)} %collective-permute-done.5.refs_3_, ...), custom_call_target="tpu_custom_call", output_to_operand_aliasing={{}: (8, {})} | custom-call | flops 1769472 | bytes 1769472 | tf_op jit(solution)/shard_map/norm0/pallas_call | solution.py:410
  (1 shorter events, 0.0 us)
Async XLA Ops:
  3.7 24.7 %all-to-all-start = ((bf16[8,160,256]{2,1,0:T(8,128)(2,1)}), bf16[8,160,256]{2,1,0:T(8,128)(2,1)}, u32[]{:S(2)}, u32[]{:S(2)}) async-start(bf16[8,160,256]{2,1,0:T(8,128)(2,1)} %tail.1), calls=%async_computation | async-start | bytes 1310720 | tf_op jit(solution)/shard_map/all_to_all | solution.py:429
  30.5 21.2 %all-to-all-start.1 = ((bf16[8,160,256]{2,1,0:T(8,128)(2,1)}), bf16[8,160,256]{2,1,0:T(8,128)(2,1)}, u32[]{:S(2)}, u32[]{:S(2)}) async-start(bf16[8,160,256]{2,1,0:T(8,128)(2,1)} %route.1), calls=%async_computation.1 | async-start | bytes 1310720 | tf_op jit(solution)/shard_map/all_to_all | solution.py:429
  42.8 3.3 %collective-permute-start.2 = (f32[1,384]{1,0:T(1,128)}, f32[1,384]{1,0:T(1,128)}, u32[]{:S(2)}, u32[]{:S(2)}) collective-permute-start(f32[1,384]{1,0:T(1,128)} %get-tuple-element.23.refs_0_), channel_id=1, source_target_pairs={{0,3},{1,2},{2,1},{3,0},{4,7},{5,6},{6,5},{7,4},{8,11},{9,10},{10,... | collective-permute-start | bytes 4616 | tf_op jit(solution)/shard_map/ppermute | solution.py:425
  43.1 3.7 %collective-permute-start.1 = (f32[1,384]{1,0:T(1,128)}, f32[1,384]{1,0:T(1,128)}, u32[]{:S(2)}, u32[]{:S(2)}) collective-permute-start(f32[1,384]{1,0:T(1,128)} %get-tuple-element.23.refs_0_), channel_id=1, source_target_pairs={{0,2},{1,3},{2,0},{3,1},{4,6},{5,7},{6,4},{7,5},{8,10},{9,11},{10,... | collective-permute-start | bytes 4616 | tf_op jit(solution)/shard_map/ppermute | solution.py:425
  44.4 2.4 %collective-permute-start = (f32[1,384]{1,0:T(1,128)}, f32[1,384]{1,0:T(1,128)}, u32[]{:S(2)}, u32[]{:S(2)}) collective-permute-start(f32[1,384]{1,0:T(1,128)} %get-tuple-element.23.refs_0_), channel_id=1, source_target_pairs={{0,1},{1,0},{2,3},{3,2},{4,5},{5,4},{6,7},{7,6},{8,9},{9,8},{10,11... | collective-permute-start | bytes 4616 | tf_op jit(solution)/shard_map/ppermute | solution.py:425
  57.6 4.9 %collective-permute-start.5 = (f32[1,256]{1,0:T(1,128)}, f32[1,256]{1,0:T(1,128)}, u32[]{:S(2)}, u32[]{:S(2)}) collective-permute-start(f32[1,256]{1,0:T(1,128)} %get-tuple-element.30.refs_0_), channel_id=1, source_target_pairs={{0,3},{1,2},{2,1},{3,0},{4,7},{5,6},{6,5},{7,4},{8,11},{9,10},{10,... | collective-permute-start | bytes 3080 | tf_op jit(solution)/shard_map/ppermute | solution.py:425
  57.6 4.8 %collective-permute-start.4 = (f32[1,256]{1,0:T(1,128)}, f32[1,256]{1,0:T(1,128)}, u32[]{:S(2)}, u32[]{:S(2)}) collective-permute-start(f32[1,256]{1,0:T(1,128)} %get-tuple-element.30.refs_0_), channel_id=1, source_target_pairs={{0,2},{1,3},{2,0},{3,1},{4,6},{5,7},{6,4},{7,5},{8,10},{9,11},{10,... | collective-permute-start | bytes 3080 | tf_op jit(solution)/shard_map/ppermute | solution.py:425
  59.2 3.3 %collective-permute-start.3 = (f32[1,256]{1,0:T(1,128)}, f32[1,256]{1,0:T(1,128)}, u32[]{:S(2)}, u32[]{:S(2)}) collective-permute-start(f32[1,256]{1,0:T(1,128)} %get-tuple-element.30.refs_0_), channel_id=1, source_target_pairs={{0,1},{1,0},{2,3},{3,2},{4,5},{5,4},{6,7},{7,6},{8,9},{9,8},{10,11... | collective-permute-start | bytes 3080 | tf_op jit(solution)/shard_map/ppermute | solution.py:425
where the time goes:
time: 66.2 us; the launch traced here: 65.5 us
  Pallas kernels  38.2 us (58%)
  starting transfers between devices  15.2 us (23%)
  waiting for transfers between devices  10.1 us (15%)
  local copies, waits for them, and re-layouts  1.28 us (2%)
  between operations  0.67 us (1%)
    all_to_all x2, starting transfers between devices, exchange(): lax.all_to_all(pieces, 'seq', split_axis=0, concat_axis=0, tiled=True)  11.5 us
    pallas_call x1, Pallas kernels, feature_call(): pl.pallas_call(feature_kernel, grid=(width // WIDE,), in_specs=[blocks[0]...  9.69 us
    pallas_call x3, Pallas kernels, norm_call(): pl.pallas_call(functools.partial(norm_kernel, channels, first_block, len(...  9.31 us
    pallas_call x1, Pallas kernels, main_call(): pl.pallas_call(functools.partial(main_kernel, group_size), grid_spec=pltp...  8.16 us
    all_to_all x2, waiting for transfers between devices, exchange(): lax.all_to_all(pieces, 'seq', split_axis=0, concat_axis=0, tiled=True)  7.94 us
    pallas_call x1, Pallas kernels, head_call(): pl.pallas_call(functools.partial(head_kernel, group_size), grid_spec=pltp...  5.88 us
    ppermute x6, starting transfers between devices, swap(): return lax.ppermute(array, axis, [(i, i ^ distance) for i in range(size)])  3.77 us
    pallas_call x1, Pallas kernels, tail_call(): pl.pallas_call(functools.partial(tail_kernel, packed), grid=(2,), in_spec...  3.11 us
  transfers between devices with their start and end apart: 8, of which 4 were waited for; matrix products, arithmetic and copies ran while one was open for 2% of the time, Pallas kernels for 37%

commit v1 on v0

--- a/solution.py
+++ b/solution.py
@@ -13,6 +13,7 @@
 LANES = 128
 STEP = 256
 WIDE = 512
+HEAD_WIDE = 1024
 SIDE = 4
 BLOCK = 32
 WINDOW = 256
@@ -286,7 +287,7 @@
         acc[...] = jnp.zeros_like(acc)
 
     def tiles():
-        for number in range(WIDE // LANES):
+        for number in range(HEAD_WIDE // LANES):
             index, tile = divmod(number, STEP // LANES)
             cols = slice(number * LANES, (number + 1) * LANES)
             here = slice(tile * LANES, (tile + 1) * LANES)
@@ -338,31 +339,31 @@
 
 def head_call(group_size, predecessor, stretch_lengths, previous, query_opening, queries, keys_in, values_in, mixed_in, residual, short_taps, lines, mixed):
     rows, width = queries.shape
-    per_step = WIDE // group_size
-    block = pl.BlockSpec((OPENING, WIDE), lambda p, *_: (0, p))
-    small = pl.BlockSpec((16, WIDE), lambda p, *_: (0, p))
+    per_step = HEAD_WIDE // group_size
+    block = pl.BlockSpec((OPENING, HEAD_WIDE), lambda p, *_: (0, p))
+    small = pl.BlockSpec((16, HEAD_WIDE), lambda p, *_: (0, p))
     return pl.pallas_call(
         functools.partial(head_kernel, group_size),
         grid_spec=pltpu.PrefetchScalarGridSpec(
             num_scalar_prefetch=2,
-            grid=(width // WIDE,),
+            grid=(width // HEAD_WIDE,),
             in_specs=[
-                pl.BlockSpec((WIDE // STEP, PACKED, STEP), lambda p, *_: (p, 0, 0)),
+                pl.BlockSpec((HEAD_WIDE // STEP, PACKED, STEP), lambda p, *_: (p, 0, 0)),
                 block,
                 small,
                 small,
                 small,
-                pl.BlockSpec((192, WIDE), lambda p, *_: (0, p)),
+                pl.BlockSpec((192, HEAD_WIDE), lambda p, *_: (0, p)),
                 block,
-                pl.BlockSpec((3, 7, WIDE), lambda p, *_: (0, 0, p)),
+                pl.BlockSpec((3, 7, HEAD_WIDE), lambda p, *_: (0, 0, p)),
                 pl.BlockSpec((per_step, WINDOW), lambda p, *_: (p, 0)),
                 pl.BlockSpec(memory_space=pl.ANY),
             ],
             out_specs=[block, pl.BlockSpec((1, 256), lambda p, *_: (0, 0))],
             scratch_shapes=[
-                pltpu.VMEM((WIDE // LANES, 24, LANES), F32),
-                pltpu.VMEM((WIDE // LANES, 24, LANES), F32),
-                pltpu.VMEM((WIDE // LANES, 24, LANES), F32),
+                pltpu.VMEM((HEAD_WIDE // LANES, 24, LANES), F32),
+                pltpu.VMEM((HEAD_WIDE // LANES, 24, LANES), F32),
+                pltpu.VMEM((HEAD_WIDE // LANES, 24, LANES), F32),
                 pltpu.VMEM((256, LANES), F32),
             ],
         ),

time: 66.2 us -> 65.3 us (0.986)
  Pallas kernels: 38.2 us -> 37.4 us
    pallas_call x1, Pallas kernels: 5.88 us -> 5.11 us  [head_call(): pl.pallas_call(functools.partial(head_kernel, group_size), grid_spec=pltp...]
where the time goes in v1:
time: 65.3 us; the launch traced here: 64.7 us
  Pallas kernels  37.4 us (57%)
  starting transfers between devices  15.2 us (23%)
  waiting for transfers between devices  10.1 us (15%)
  local copies, waits for them, and re-layouts  1.28 us (2%)
  between operations  0.67 us (1%)
    all_to_all x2, starting transfers between devices, exchange(): lax.all_to_all(pieces, 'seq', split_axis=0, concat_axis=0, tiled=True)  11.5 us
    pallas_call x1, Pallas kernels, feature_call(): pl.pallas_call(feature_kernel, grid=(width // WIDE,), in_specs=[blocks[0]...  9.69 us
    pallas_call x3, Pallas kernels, norm_call(): pl.pallas_call(functools.partial(norm_kernel, channels, first_block, len(...  9.31 us
    pallas_call x1, Pallas kernels, main_call(): pl.pallas_call(functools.partial(main_kernel, group_size), grid_spec=pltp...  8.16 us
    all_to_all x2, waiting for transfers between devices, exchange(): lax.all_to_all(pieces, 'seq', split_axis=0, concat_axis=0, tiled=True)  7.94 us
    pallas_call x1, Pallas kernels, head_call(): pl.pallas_call(functools.partial(head_kernel, group_size), grid_spec=pltp...  5.11 us
    ppermute x6, starting transfers between devices, swap(): return lax.ppermute(array, axis, [(i, i ^ distance) for i in range(size)])  3.76 us
    pallas_call x1, Pallas kernels, tail_call(): pl.pallas_call(functools.partial(tail_kernel, packed), grid=(2,), in_spec...  3.11 us
  transfers between devices with their start and end apart: 8, of which 4 were waited for; matrix products, arithmetic and copies ran while one was open for 2% of the time, Pallas kernels for 37%

profile of v1, /device:TPU:0, one launch (start us, length us, event | category | flops | bytes accessed | tf_op | source)
XLA Modules:
  0.0 64.7 jit_solution(16220302330571933530)
XLA Ops:
  0.6 3.1 %tail.1 = bf16[8,160,256]{2,1,0:T(8,128)(2,1)} custom-call(bf16[512,2048]{1,0:T(8,128)(2,1)} %q_ref.5, bf16[512,2048]{1,0:T(8,128)(2,1)} %k_ref.5, bf16[512,2048]{1,0:T(8,128)(2,1)} %v_ref.5, bf16[512,2048]{1,0:T(8,128)(2,1)} %k_ref.5, bf16[512,2048]{1,0:T(8,128)(2,1)} %v_ref.5, bf16[3,7,2048]{2,1,0:T(8,128)(2,1)} %taps_ref.5, bf16[16,128]{1,0:T(8,128)(2,1)} %filt_ref.1), custom_call_target="tpu_custom_call" | custom-call | flops 7864320 | bytes 1572864 | tf_op jit(solution)/shard_map/tail/pallas_call | solution.py:77
  3.7 7.3 %all-to-all-start = ((bf16[8,160,256]{2,1,0:T(8,128)(2,1)}), bf16[8,160,256]{2,1,0:T(8,128)(2,1)}, u32[]{:S(2)}, u32[]{:S(2)}) async-start(bf16[8,160,256]{2,1,0:T(8,128)(2,1)} %tail.1), calls=%async_computation | async-start | bytes 1310720 | tf_op jit(solution)/shard_map/all_to_all | solution.py:430
  11.0 1.3 %reshape.7.refs_6_ = bf16[1,2048]{1,0:T(2,128)(2,1)} reshape(bf16[2048]{0:T(1024)(128)(2,1)} %param.15) | data formatting | bytes 8192 | tf_op jit(solution)/shard_map/reshape | solution.py:446
  12.3 9.7 %features.1 = (bf16[512,2048]{1,0:T(8,128)(2,1)}, f32[144,2048]{1,0:T(8,128)}, f32[384,2048]{1,0:T(8,128)}) custom-call(bf16[512,2048]{1,0:T(8,128)(2,1)} %q_ref.5, bf16[512,2048]{1,0:T(8,128)(2,1)} %k_ref.5, bf16[512,2048]{1,0:T(8,128)(2,1)} %v_ref.5, bf16[3,7,2048]{2,1,0:T(8,128)(2,1)} %taps_ref.5), custom_call_target="tpu_custom_call" | custom-call | flops 47185920 | bytes 13631488 | tf_op jit(solution)/shard_map/features/pallas_call | solution.py:127
  22.0 6.4 %all-to-all-done.in_ref.filt_ref = bf16[8,160,256]{2,1,0:T(8,128)(2,1)} async-done(((bf16[8,160,256]{2,1,0:T(8,128)(2,1)}), bf16[8,160,256]{2,1,0:T(8,128)(2,1)}, u32[]{:S(2)}, u32[]{:S(2)}) %all-to-all-start) | async-done | bytes 655392 | tf_op jit(solution)/shard_map/all_to_all | solution.py:430
  28.4 2.0 %route.1 = bf16[8,160,256]{2,1,0:T(8,128)(2,1)} custom-call(s32[8]{0:T(128)} %pred_ref.3, bf16[8,160,256]{2,1,0:T(8,128)(2,1)} %all-to-all-done.in_ref.filt_ref), custom_call_target="tpu_custom_call" | custom-call | bytes 1310720 | tf_op jit(solution)/shard_map/route/pallas_call | solution.py:148
  30.5 4.2 %all-to-all-start.1 = ((bf16[8,160,256]{2,1,0:T(8,128)(2,1)}), bf16[8,160,256]{2,1,0:T(8,128)(2,1)}, u32[]{:S(2)}, u32[]{:S(2)}) async-start(bf16[8,160,256]{2,1,0:T(8,128)(2,1)} %route.1), calls=%async_computation.1 | async-start | bytes 1310720 | tf_op jit(solution)/shard_map/all_to_all | solution.py:430
  34.7 8.2 %conv.1 = (bf16[512,2048]{1,0:T(8,128)(2,1)}, f32[1,384]{1,0:T(1,128)}, f32[128,256]{1,0:T(8,128)}) custom-call(s32[8]{0:T(128)} %len_ref.9, f32[384,2048]{1,0:T(8,128)} %get-tuple-element.20.query_ref, bf16[512,2048]{1,0:T(8,128)(2,1)} %get-tuple-element.21.u_ref, bf16[512,2048]{1,0:T(8,128)(2,1)} %refs_5_.5, bf16[8,160,256]{2,1,0:T(8,128)(2,1)} %all-to-all-done.in_ref.filt_ref), custom_call_target="tpu_custom_call" | custom-call | flops 4294967296 | bytes 12582912 | tf_op jit(solution)/shard_map/conv/pallas_call | solution.py:246
  42.8 0.3 collective-permute-start.2
  43.1 1.3 %collective-permute-start.1 = (f32[1,384]{1,0:T(1,128)}, f32[1,384]{1,0:T(1,128)}, u32[]{:S(2)}, u32[]{:S(2)}) collective-permute-start(f32[1,384]{1,0:T(1,128)} %get-tuple-element.23.refs_0_), channel_id=1, source_target_pairs={{0,2},{1,3},{2,0},{3,1},{4,6},{5,7},{6,4},{7,5},{8,10},{9,11},{10,... | collective-permute-start | bytes 4616 | tf_op jit(solution)/shard_map/ppermute | solution.py:426
  44.4 0.3 collective-permute-start
  44.7 1.5 %collective-permute-done.2.refs_3_ = f32[1,384]{1,0:T(1,128)} collective-permute-done((f32[1,384]{1,0:T(1,128)}, f32[1,384]{1,0:T(1,128)}, u32[]{:S(2)}, u32[]{:S(2)}) %collective-permute-start.2) | collective-permute-done | bytes 1568 | tf_op jit(solution)/shard_map/ppermute | solution.py:426
  46.1 0.7 %collective-permute-done.1.refs_2_ = f32[1,384]{1,0:T(1,128)} collective-permute-done((f32[1,384]{1,0:T(1,128)}, f32[1,384]{1,0:T(1,128)}, u32[]{:S(2)}, u32[]{:S(2)}) %collective-permute-start.1) | collective-permute-done | bytes 1568 | tf_op jit(solution)/shard_map/ppermute | solution.py:426
  46.8 0.0 collective-permute-done.refs_1_
  46.8 3.3 %norm1.1.refs_7_ = bf16[512,2048]{1,0:T(8,128)(2,1)} custom-call(s32[8]{0:T(128)} %len_ref.9, f32[1,384]{1,0:T(1,128)} %get-tuple-element.23.refs_0_, f32[1,384]{1,0:T(1,128)} %collective-permute-done.refs_1_, f32[1,384]{1,0:T(1,128)} %collective-permute-done.1.refs_2_, f32[1,384]{1,0:T(1,128)} %collective-permute-done.2.refs_3_, ...), custom_call_target="tpu_custom_call" | custom-call | flops 3145728 | bytes 3145728 | tf_op jit(solution)/shard_map/norm1/pallas_call | solution.py:411
  50.2 1.5 %all-to-all-done.1.held = bf16[8,160,256]{2,1,0:T(8,128)(2,1)} async-done(((bf16[8,160,256]{2,1,0:T(8,128)(2,1)}), bf16[8,160,256]{2,1,0:T(8,128)(2,1)}, u32[]{:S(2)}, u32[]{:S(2)}) %all-to-all-start.1) | async-done | bytes 655392 | tf_op jit(solution)/shard_map/all_to_all | solution.py:430
  51.7 5.1 %head.1 = (bf16[512,2048]{1,0:T(8,128)(2,1)}, f32[1,256]{1,0:T(1,128)}) custom-call(s32[8]{0:T(128)} %pred_ref.3, s32[8]{0:T(128)} %len_ref.9, bf16[8,160,256]{2,1,0:T(8,128)(2,1)} %all-to-all-done.1.held, f32[144,2048]{1,0:T(8,128)} %get-tuple-element.27.query_ref, bf16[512,2048]{1,0:T(8,128)(2,1)} %q_ref.5, ...), custom_call_target="tpu_custom_call", output_to_operand_aliasing={{0}: (11, {})} | custom-call | flops 1073741824 | bytes 3145728 | tf_op jit(solution)/shard_map/head/pallas_call | solution.py:345
  56.8 0.1 collective-permute-start.5
  56.9 1.5 %collective-permute-start.4 = (f32[1,256]{1,0:T(1,128)}, f32[1,256]{1,0:T(1,128)}, u32[]{:S(2)}, u32[]{:S(2)}) collective-permute-start(f32[1,256]{1,0:T(1,128)} %get-tuple-element.30.refs_0_), channel_id=1, source_target_pairs={{0,2},{1,3},{2,0},{3,1},{4,6},{5,7},{6,4},{7,5},{8,10},{9,11},{10,... | collective-permute-start | bytes 3080 | tf_op jit(solution)/shard_map/ppermute | solution.py:426
  58.4 0.3 collective-permute-start.3
  58.7 3.0 %norm3.1.refs_7_ = bf16[512,2048]{1,0:T(8,128)(2,1)} custom-call(s32[8]{0:T(128)} %len_ref.9, f32[1,384]{1,0:T(1,128)} %get-tuple-element.23.refs_0_, f32[1,384]{1,0:T(1,128)} %collective-permute-done.refs_1_, f32[1,384]{1,0:T(1,128)} %collective-permute-done.1.refs_2_, f32[1,384]{1,0:T(1,128)} %collective-permute-done.2.refs_3_, ...), custom_call_target="tpu_custom_call", output_to_operand_aliasing={{}: (8, {})} | custom-call | flops 1572864 | bytes 1572864 | tf_op jit(solution)/shard_map/norm3/pallas_call | solution.py:411
  61.7 0.0 collective-permute-done.5.refs_3_
  61.7 0.0 collective-permute-done.4.refs_2_
  61.7 3.0 %norm0.1 = bf16[512,2048]{1,0:T(8,128)(2,1)} custom-call(s32[8]{0:T(128)} %len_ref.9, f32[1,256]{1,0:T(1,128)} %get-tuple-element.30.refs_0_, f32[1,256]{1,0:T(1,128)} %collective-permute-done.3.refs_1_, f32[1,256]{1,0:T(1,128)} %collective-permute-done.4.refs_2_, f32[1,256]{1,0:T(1,128)} %collective-permute-done.5.refs_3_, ...), custom_call_target="tpu_custom_call", output_to_operand_aliasing={{}: (8, {})} | custom-call | flops 1769472 | bytes 1769472 | tf_op jit(solution)/shard_map/norm0/pallas_call | solution.py:411
  (1 shorter events, 0.0 us)
Async XLA Ops:
  3.7 24.7 %all-to-all-start = ((bf16[8,160,256]{2,1,0:T(8,128)(2,1)}), bf16[8,160,256]{2,1,0:T(8,128)(2,1)}, u32[]{:S(2)}, u32[]{:S(2)}) async-start(bf16[8,160,256]{2,1,0:T(8,128)(2,1)} %tail.1), calls=%async_computation | async-start | bytes 1310720 | tf_op jit(solution)/shard_map/all_to_all | solution.py:430
  30.5 21.2 %all-to-all-start.1 = ((bf16[8,160,256]{2,1,0:T(8,128)(2,1)}), bf16[8,160,256]{2,1,0:T(8,128)(2,1)}, u32[]{:S(2)}, u32[]{:S(2)}) async-start(bf16[8,160,256]{2,1,0:T(8,128)(2,1)} %route.1), calls=%async_computation.1 | async-start | bytes 1310720 | tf_op jit(solution)/shard_map/all_to_all | solution.py:430
  42.8 3.3 %collective-permute-start.2 = (f32[1,384]{1,0:T(1,128)}, f32[1,384]{1,0:T(1,128)}, u32[]{:S(2)}, u32[]{:S(2)}) collective-permute-start(f32[1,384]{1,0:T(1,128)} %get-tuple-element.23.refs_0_), channel_id=1, source_target_pairs={{0,3},{1,2},{2,1},{3,0},{4,7},{5,6},{6,5},{7,4},{8,11},{9,10},{10,... | collective-permute-start | bytes 4616 | tf_op jit(solution)/shard_map/ppermute | solution.py:426
  43.1 3.7 %collective-permute-start.1 = (f32[1,384]{1,0:T(1,128)}, f32[1,384]{1,0:T(1,128)}, u32[]{:S(2)}, u32[]{:S(2)}) collective-permute-start(f32[1,384]{1,0:T(1,128)} %get-tuple-element.23.refs_0_), channel_id=1, source_target_pairs={{0,2},{1,3},{2,0},{3,1},{4,6},{5,7},{6,4},{7,5},{8,10},{9,11},{10,... | collective-permute-start | bytes 4616 | tf_op jit(solution)/shard_map/ppermute | solution.py:426
  44.4 2.4 %collective-permute-start = (f32[1,384]{1,0:T(1,128)}, f32[1,384]{1,0:T(1,128)}, u32[]{:S(2)}, u32[]{:S(2)}) collective-permute-start(f32[1,384]{1,0:T(1,128)} %get-tuple-element.23.refs_0_), channel_id=1, source_target_pairs={{0,1},{1,0},{2,3},{3,2},{4,5},{5,4},{6,7},{7,6},{8,9},{9,8},{10,11... | collective-permute-start | bytes 4616 | tf_op jit(solution)/shard_map/ppermute | solution.py:426
  56.8 4.9 %collective-permute-start.5 = (f32[1,256]{1,0:T(1,128)}, f32[1,256]{1,0:T(1,128)}, u32[]{:S(2)}, u32[]{:S(2)}) collective-permute-start(f32[1,256]{1,0:T(1,128)} %get-tuple-element.30.refs_0_), channel_id=1, source_target_pairs={{0,3},{1,2},{2,1},{3,0},{4,7},{5,6},{6,5},{7,4},{8,11},{9,10},{10,... | collective-permute-start | bytes 3080 | tf_op jit(solution)/shard_map/ppermute | solution.py:426
  56.9 4.8 %collective-permute-start.4 = (f32[1,256]{1,0:T(1,128)}, f32[1,256]{1,0:T(1,128)}, u32[]{:S(2)}, u32[]{:S(2)}) collective-permute-start(f32[1,256]{1,0:T(1,128)} %get-tuple-element.30.refs_0_), channel_id=1, source_target_pairs={{0,2},{1,3},{2,0},{3,1},{4,6},{5,7},{6,4},{7,5},{8,10},{9,11},{10,... | collective-permute-start | bytes 3080 | tf_op jit(solution)/shard_map/ppermute | solution.py:426
  58.4 3.3 %collective-permute-start.3 = (f32[1,256]{1,0:T(1,128)}, f32[1,256]{1,0:T(1,128)}, u32[]{:S(2)}, u32[]{:S(2)}) collective-permute-start(f32[1,256]{1,0:T(1,128)} %get-tuple-element.30.refs_0_), channel_id=1, source_target_pairs={{0,1},{1,0},{2,3},{3,2},{4,5},{5,4},{6,7},{7,6},{8,9},{9,8},{10,11... | collective-permute-start | bytes 3080 | tf_op jit(solution)/shard_map/ppermute | solution.py:426

commit v2 on v0

--- a/solution.py
+++ b/solution.py
@@ -13,6 +13,7 @@
 LANES = 128
 STEP = 256
 WIDE = 512
+BROAD = 1024
 SIDE = 4
 BLOCK = 32
 WINDOW = 256
@@ -202,9 +203,9 @@
         acc[...] = jnp.zeros_like(acc)
 
     def tiles():
-        for number in range(WIDE // LANES):
+        for number in range(BROAD // LANES):
             cols = slice(number * LANES, (number + 1) * LANES)
-            base = pl.multiple_of((step * (WIDE // LANES) + number) * per_lane, per_lane)
+            base = pl.multiple_of((step * (BROAD // LANES) + number) * per_lane, per_lane)
             matrix = toeplitz(lines_ref[pl.ds(base, per_lane), :])
             for start in range(128, rows, SIDE * BLOCK):
                 windows = []
@@ -240,15 +241,15 @@
         filter_spec = pl.BlockSpec(filter_rows.shape, lambda p, *_: (0, 0))
     else:
         filter_spec = pl.BlockSpec((filter_rows.shape[0], 16, STEP), lambda p, *_: (0, PACKED // 16 - 1, 0))
-    block = pl.BlockSpec((rows, WIDE), lambda p, *_: (0, p))
-    later = pl.BlockSpec((pl.Element(rows - 128), pl.Element(WIDE)), lambda p, *_: (128, p * WIDE))
+    block = pl.BlockSpec((rows, BROAD), lambda p, *_: (0, p))
+    later = pl.BlockSpec((pl.Element(rows - 128), pl.Element(BROAD)), lambda p, *_: (128, p * BROAD))
     return pl.pallas_call(
         functools.partial(main_kernel, group_size),
         grid_spec=pltpu.PrefetchScalarGridSpec(
             num_scalar_prefetch=1,
-            grid=(width // WIDE,),
+            grid=(width // BROAD,),
             in_specs=[
-                pl.BlockSpec((rows - 128, WIDE), lambda p, *_: (0, p)),
+                pl.BlockSpec((rows - 128, BROAD), lambda p, *_: (0, p)),
                 block,
                 later,
                 filter_spec,
@@ -286,7 +287,7 @@
         acc[...] = jnp.zeros_like(acc)
 
     def tiles():
-        for number in range(WIDE // LANES):
+        for number in range(BROAD // LANES):
             index, tile = divmod(number, STEP // LANES)
             cols = slice(number * LANES, (number + 1) * LANES)
             here = slice(tile * LANES, (tile + 1) * LANES)
@@ -338,31 +339,31 @@
 
 def head_call(group_size, predecessor, stretch_lengths, previous, query_opening, queries, keys_in, values_in, mixed_in, residual, short_taps, lines, mixed):
     rows, width = queries.shape
-    per_step = WIDE // group_size
-    block = pl.BlockSpec((OPENING, WIDE), lambda p, *_: (0, p))
-    small = pl.BlockSpec((16, WIDE), lambda p, *_: (0, p))
+    per_step = BROAD // group_size
+    block = pl.BlockSpec((OPENING, BROAD), lambda p, *_: (0, p))
+    small = pl.BlockSpec((16, BROAD), lambda p, *_: (0, p))
     return pl.pallas_call(
         functools.partial(head_kernel, group_size),
         grid_spec=pltpu.PrefetchScalarGridSpec(
             num_scalar_prefetch=2,
-            grid=(width // WIDE,),
+            grid=(width // BROAD,),
             in_specs=[
-                pl.BlockSpec((WIDE // STEP, PACKED, STEP), lambda p, *_: (p, 0, 0)),
+                pl.BlockSpec((BROAD // STEP, PACKED, STEP), lambda p, *_: (p, 0, 0)),
                 block,
                 small,
                 small,
                 small,
-                pl.BlockSpec((192, WIDE), lambda p, *_: (0, p)),
+                pl.BlockSpec((192, BROAD), lambda p, *_: (0, p)),
                 block,
-                pl.BlockSpec((3, 7, WIDE), lambda p, *_: (0, 0, p)),
+                pl.BlockSpec((3, 7, BROAD), lambda p, *_: (0, 0, p)),
                 pl.BlockSpec((per_step, WINDOW), lambda p, *_: (p, 0)),
                 pl.BlockSpec(memory_space=pl.ANY),
             ],
             out_specs=[block, pl.BlockSpec((1, 256), lambda p, *_: (0, 0))],
             scratch_shapes=[
-                pltpu.VMEM((WIDE // LANES, 24, LANES), F32),
-                pltpu.VMEM((WIDE // LANES, 24, LANES), F32),
-                pltpu.VMEM((WIDE // LANES, 24, LANES), F32),
+                pltpu.VMEM((BROAD // LANES, 24, LANES), F32),
+                pltpu.VMEM((BROAD // LANES, 24, LANES), F32),
+                pltpu.VMEM((BROAD // LANES, 24, LANES), F32),
                 pltpu.VMEM((256, LANES), F32),
             ],
         ),

time: 66.2 us -> 65.3 us (0.986)
  Pallas kernels: 38.2 us -> 37.1 us
    pallas_call x1, Pallas kernels: 5.88 us -> 5.11 us  [head_call(): pl.pallas_call(functools.partial(head_kernel, group_size), grid_spec=pltp...]
where the time goes in v2:
time: 65.3 us; the launch traced here: 64.7 us
  Pallas kernels  37.1 us (57%)
  starting transfers between devices  15.2 us (23%)
  waiting for transfers between devices  10.4 us (16%)
  local copies, waits for them, and re-layouts  1.28 us (2%)
  between operations  0.67 us (1%)
    all_to_all x2, starting transfers between devices, exchange(): lax.all_to_all(pieces, 'seq', split_axis=0, concat_axis=0, tiled=True)  11.5 us
    pallas_call x1, Pallas kernels, feature_call(): pl.pallas_call(feature_kernel, grid=(width // WIDE,), in_specs=[blocks[0]...  9.69 us
    pallas_call x3, Pallas kernels, norm_call(): pl.pallas_call(functools.partial(norm_kernel, channels, first_block, len(...  9.31 us
    all_to_all x2, waiting for transfers between devices, exchange(): lax.all_to_all(pieces, 'seq', split_axis=0, concat_axis=0, tiled=True)  8.26 us
    pallas_call x1, Pallas kernels, main_call(): pl.pallas_call(functools.partial(main_kernel, group_size), grid_spec=pltp...  7.83 us
    pallas_call x1, Pallas kernels, head_call(): pl.pallas_call(functools.partial(head_kernel, group_size), grid_spec=pltp...  5.11 us
    ppermute x6, starting transfers between devices, swap(): return lax.ppermute(array, axis, [(i, i ^ distance) for i in range(size)])  3.76 us
    pallas_call x1, Pallas kernels, tail_call(): pl.pallas_call(functools.partial(tail_kernel, packed), grid=(2,), in_spec...  3.11 us
  transfers between devices with their start and end apart: 8, of which 4 were waited for; matrix products, arithmetic and copies ran while one was open for 2% of the time, Pallas kernels for 37%

profile of v2, /device:TPU:0, one launch (start us, length us, event | category | flops | bytes accessed | tf_op | source)
XLA Modules:
  0.0 64.7 jit_solution(17546187031480783600)
XLA Ops:
  0.6 3.1 %tail.1 = bf16[8,160,256]{2,1,0:T(8,128)(2,1)} custom-call(bf16[512,2048]{1,0:T(8,128)(2,1)} %q_ref.5, bf16[512,2048]{1,0:T(8,128)(2,1)} %k_ref.5, bf16[512,2048]{1,0:T(8,128)(2,1)} %v_ref.5, bf16[512,2048]{1,0:T(8,128)(2,1)} %k_ref.5, bf16[512,2048]{1,0:T(8,128)(2,1)} %v_ref.5, bf16[3,7,2048]{2,1,0:T(8,128)(2,1)} %taps_ref.5, bf16[16,128]{1,0:T(8,128)(2,1)} %filt_ref.1), custom_call_target="tpu_custom_call" | custom-call | flops 7864320 | bytes 1572864 | tf_op jit(solution)/shard_map/tail/pallas_call | solution.py:77
  3.7 7.3 %all-to-all-start = ((bf16[8,160,256]{2,1,0:T(8,128)(2,1)}), bf16[8,160,256]{2,1,0:T(8,128)(2,1)}, u32[]{:S(2)}, u32[]{:S(2)}) async-start(bf16[8,160,256]{2,1,0:T(8,128)(2,1)} %tail.1), calls=%async_computation | async-start | bytes 1310720 | tf_op jit(solution)/shard_map/all_to_all | solution.py:430
  11.0 1.3 %reshape.7.refs_6_ = bf16[1,2048]{1,0:T(2,128)(2,1)} reshape(bf16[2048]{0:T(1024)(128)(2,1)} %param.15) | data formatting | bytes 8192 | tf_op jit(solution)/shard_map/reshape | solution.py:446
  12.3 9.7 %features.1 = (bf16[512,2048]{1,0:T(8,128)(2,1)}, f32[144,2048]{1,0:T(8,128)}, f32[384,2048]{1,0:T(8,128)}) custom-call(bf16[512,2048]{1,0:T(8,128)(2,1)} %q_ref.5, bf16[512,2048]{1,0:T(8,128)(2,1)} %k_ref.5, bf16[512,2048]{1,0:T(8,128)(2,1)} %v_ref.5, bf16[3,7,2048]{2,1,0:T(8,128)(2,1)} %taps_ref.5), custom_call_target="tpu_custom_call" | custom-call | flops 47185920 | bytes 13631488 | tf_op jit(solution)/shard_map/features/pallas_call | solution.py:127
  22.0 6.4 %all-to-all-done.in_ref.filt_ref = bf16[8,160,256]{2,1,0:T(8,128)(2,1)} async-done(((bf16[8,160,256]{2,1,0:T(8,128)(2,1)}), bf16[8,160,256]{2,1,0:T(8,128)(2,1)}, u32[]{:S(2)}, u32[]{:S(2)}) %all-to-all-start) | async-done | bytes 655392 | tf_op jit(solution)/shard_map/all_to_all | solution.py:430
  28.4 2.0 %route.1 = bf16[8,160,256]{2,1,0:T(8,128)(2,1)} custom-call(s32[8]{0:T(128)} %pred_ref.3, bf16[8,160,256]{2,1,0:T(8,128)(2,1)} %all-to-all-done.in_ref.filt_ref), custom_call_target="tpu_custom_call" | custom-call | bytes 1310720 | tf_op jit(solution)/shard_map/route/pallas_call | solution.py:148
  30.5 4.2 %all-to-all-start.1 = ((bf16[8,160,256]{2,1,0:T(8,128)(2,1)}), bf16[8,160,256]{2,1,0:T(8,128)(2,1)}, u32[]{:S(2)}, u32[]{:S(2)}) async-start(bf16[8,160,256]{2,1,0:T(8,128)(2,1)} %route.1), calls=%async_computation.1 | async-start | bytes 1310720 | tf_op jit(solution)/shard_map/all_to_all | solution.py:430
  34.7 7.8 %conv.1 = (bf16[512,2048]{1,0:T(8,128)(2,1)}, f32[1,384]{1,0:T(1,128)}, f32[128,256]{1,0:T(8,128)}) custom-call(s32[8]{0:T(128)} %len_ref.9, f32[384,2048]{1,0:T(8,128)} %get-tuple-element.20.query_ref, bf16[512,2048]{1,0:T(8,128)(2,1)} %get-tuple-element.21.u_ref, bf16[512,2048]{1,0:T(8,128)(2,1)} %refs_5_.5, bf16[8,160,256]{2,1,0:T(8,128)(2,1)} %all-to-all-done.in_ref.filt_ref), custom_call_target="tpu_custom_call" | custom-call | flops 4294967296 | bytes 12582912 | tf_op jit(solution)/shard_map/conv/pallas_call | solution.py:246
  42.5 0.3 collective-permute-start.2
  42.8 1.3 %collective-permute-start.1 = (f32[1,384]{1,0:T(1,128)}, f32[1,384]{1,0:T(1,128)}, u32[]{:S(2)}, u32[]{:S(2)}) collective-permute-start(f32[1,384]{1,0:T(1,128)} %get-tuple-element.23.refs_0_), channel_id=1, source_target_pairs={{0,2},{1,3},{2,0},{3,1},{4,6},{5,7},{6,4},{7,5},{8,10},{9,11},{10,... | collective-permute-start | bytes 4616 | tf_op jit(solution)/shard_map/ppermute | solution.py:426
  44.1 0.3 collective-permute-start
  44.4 1.5 %collective-permute-done.2.refs_3_ = f32[1,384]{1,0:T(1,128)} collective-permute-done((f32[1,384]{1,0:T(1,128)}, f32[1,384]{1,0:T(1,128)}, u32[]{:S(2)}, u32[]{:S(2)}) %collective-permute-start.2) | collective-permute-done | bytes 1568 | tf_op jit(solution)/shard_map/ppermute | solution.py:426
  45.8 0.7 %collective-permute-done.1.refs_2_ = f32[1,384]{1,0:T(1,128)} collective-permute-done((f32[1,384]{1,0:T(1,128)}, f32[1,384]{1,0:T(1,128)}, u32[]{:S(2)}, u32[]{:S(2)}) %collective-permute-start.1) | collective-permute-done | bytes 1568 | tf_op jit(solution)/shard_map/ppermute | solution.py:426
  46.5 0.0 collective-permute-done.refs_1_
  46.5 3.3 %norm1.1.refs_7_ = bf16[512,2048]{1,0:T(8,128)(2,1)} custom-call(s32[8]{0:T(128)} %len_ref.9, f32[1,384]{1,0:T(1,128)} %get-tuple-element.23.refs_0_, f32[1,384]{1,0:T(1,128)} %collective-permute-done.refs_1_, f32[1,384]{1,0:T(1,128)} %collective-permute-done.1.refs_2_, f32[1,384]{1,0:T(1,128)} %collective-permute-done.2.refs_3_, ...), custom_call_target="tpu_custom_call" | custom-call | flops 3145728 | bytes 3145728 | tf_op jit(solution)/shard_map/norm1/pallas_call | solution.py:411
  49.8 1.8 %all-to-all-done.1.held = bf16[8,160,256]{2,1,0:T(8,128)(2,1)} async-done(((bf16[8,160,256]{2,1,0:T(8,128)(2,1)}), bf16[8,160,256]{2,1,0:T(8,128)(2,1)}, u32[]{:S(2)}, u32[]{:S(2)}) %all-to-all-start.1) | async-done | bytes 655392 | tf_op jit(solution)/shard_map/all_to_all | solution.py:430
  51.7 5.1 %head.1 = (bf16[512,2048]{1,0:T(8,128)(2,1)}, f32[1,256]{1,0:T(1,128)}) custom-call(s32[8]{0:T(128)} %pred_ref.3, s32[8]{0:T(128)} %len_ref.9, bf16[8,160,256]{2,1,0:T(8,128)(2,1)} %all-to-all-done.1.held, f32[144,2048]{1,0:T(8,128)} %get-tuple-element.27.query_ref, bf16[512,2048]{1,0:T(8,128)(2,1)} %q_ref.5, ...), custom_call_target="tpu_custom_call", output_to_operand_aliasing={{0}: (11, {})} | custom-call | flops 1073741824 | bytes 3145728 | tf_op jit(solution)/shard_map/head/pallas_call | solution.py:345
  56.8 0.1 collective-permute-start.5
  56.9 1.5 %collective-permute-start.4 = (f32[1,256]{1,0:T(1,128)}, f32[1,256]{1,0:T(1,128)}, u32[]{:S(2)}, u32[]{:S(2)}) collective-permute-start(f32[1,256]{1,0:T(1,128)} %get-tuple-element.30.refs_0_), channel_id=1, source_target_pairs={{0,2},{1,3},{2,0},{3,1},{4,6},{5,7},{6,4},{7,5},{8,10},{9,11},{10,... | collective-permute-start | bytes 3080 | tf_op jit(solution)/shard_map/ppermute | solution.py:426
  58.4 0.3 collective-permute-start.3
  58.7 3.0 %norm3.1.refs_7_ = bf16[512,2048]{1,0:T(8,128)(2,1)} custom-call(s32[8]{0:T(128)} %len_ref.9, f32[1,384]{1,0:T(1,128)} %get-tuple-element.23.refs_0_, f32[1,384]{1,0:T(1,128)} %collective-permute-done.refs_1_, f32[1,384]{1,0:T(1,128)} %collective-permute-done.1.refs_2_, f32[1,384]{1,0:T(1,128)} %collective-permute-done.2.refs_3_, ...), custom_call_target="tpu_custom_call", output_to_operand_aliasing={{}: (8, {})} | custom-call | flops 1572864 | bytes 1572864 | tf_op jit(solution)/shard_map/norm3/pallas_call | solution.py:411
  61.7 0.0 collective-permute-done.5.refs_3_
  61.7 0.0 collective-permute-done.4.refs_2_
  61.7 3.0 %norm0.1 = bf16[512,2048]{1,0:T(8,128)(2,1)} custom-call(s32[8]{0:T(128)} %len_ref.9, f32[1,256]{1,0:T(1,128)} %get-tuple-element.30.refs_0_, f32[1,256]{1,0:T(1,128)} %collective-permute-done.3.refs_1_, f32[1,256]{1,0:T(1,128)} %collective-permute-done.4.refs_2_, f32[1,256]{1,0:T(1,128)} %collective-permute-done.5.refs_3_, ...), custom_call_target="tpu_custom_call", output_to_operand_aliasing={{}: (8, {})} | custom-call | flops 1769472 | bytes 1769472 | tf_op jit(solution)/shard_map/norm0/pallas_call | solution.py:411
  (1 shorter events, 0.0 us)
Async XLA Ops:
  3.7 24.7 %all-to-all-start = ((bf16[8,160,256]{2,1,0:T(8,128)(2,1)}), bf16[8,160,256]{2,1,0:T(8,128)(2,1)}, u32[]{:S(2)}, u32[]{:S(2)}) async-start(bf16[8,160,256]{2,1,0:T(8,128)(2,1)} %tail.1), calls=%async_computation | async-start | bytes 1310720 | tf_op jit(solution)/shard_map/all_to_all | solution.py:430
  30.5 21.2 %all-to-all-start.1 = ((bf16[8,160,256]{2,1,0:T(8,128)(2,1)}), bf16[8,160,256]{2,1,0:T(8,128)(2,1)}, u32[]{:S(2)}, u32[]{:S(2)}) async-start(bf16[8,160,256]{2,1,0:T(8,128)(2,1)} %route.1), calls=%async_computation.1 | async-start | bytes 1310720 | tf_op jit(solution)/shard_map/all_to_all | solution.py:430
  42.5 3.3 %collective-permute-start.2 = (f32[1,384]{1,0:T(1,128)}, f32[1,384]{1,0:T(1,128)}, u32[]{:S(2)}, u32[]{:S(2)}) collective-permute-start(f32[1,384]{1,0:T(1,128)} %get-tuple-element.23.refs_0_), channel_id=1, source_target_pairs={{0,3},{1,2},{2,1},{3,0},{4,7},{5,6},{6,5},{7,4},{8,11},{9,10},{10,... | collective-permute-start | bytes 4616 | tf_op jit(solution)/shard_map/ppermute | solution.py:426
  42.8 3.7 %collective-permute-start.1 = (f32[1,384]{1,0:T(1,128)}, f32[1,384]{1,0:T(1,128)}, u32[]{:S(2)}, u32[]{:S(2)}) collective-permute-start(f32[1,384]{1,0:T(1,128)} %get-tuple-element.23.refs_0_), channel_id=1, source_target_pairs={{0,2},{1,3},{2,0},{3,1},{4,6},{5,7},{6,4},{7,5},{8,10},{9,11},{10,... | collective-permute-start | bytes 4616 | tf_op jit(solution)/shard_map/ppermute | solution.py:426
  44.1 2.4 %collective-permute-start = (f32[1,384]{1,0:T(1,128)}, f32[1,384]{1,0:T(1,128)}, u32[]{:S(2)}, u32[]{:S(2)}) collective-permute-start(f32[1,384]{1,0:T(1,128)} %get-tuple-element.23.refs_0_), channel_id=1, source_target_pairs={{0,1},{1,0},{2,3},{3,2},{4,5},{5,4},{6,7},{7,6},{8,9},{9,8},{10,11... | collective-permute-start | bytes 4616 | tf_op jit(solution)/shard_map/ppermute | solution.py:426
  56.8 4.9 %collective-permute-start.5 = (f32[1,256]{1,0:T(1,128)}, f32[1,256]{1,0:T(1,128)}, u32[]{:S(2)}, u32[]{:S(2)}) collective-permute-start(f32[1,256]{1,0:T(1,128)} %get-tuple-element.30.refs_0_), channel_id=1, source_target_pairs={{0,3},{1,2},{2,1},{3,0},{4,7},{5,6},{6,5},{7,4},{8,11},{9,10},{10,... | collective-permute-start | bytes 3080 | tf_op jit(solution)/shard_map/ppermute | solution.py:426
  56.9 4.8 %collective-permute-start.4 = (f32[1,256]{1,0:T(1,128)}, f32[1,256]{1,0:T(1,128)}, u32[]{:S(2)}, u32[]{:S(2)}) collective-permute-start(f32[1,256]{1,0:T(1,128)} %get-tuple-element.30.refs_0_), channel_id=1, source_target_pairs={{0,2},{1,3},{2,0},{3,1},{4,6},{5,7},{6,4},{7,5},{8,10},{9,11},{10,... | collective-permute-start | bytes 3080 | tf_op jit(solution)/shard_map/ppermute | solution.py:426
  58.4 3.3 %collective-permute-start.3 = (f32[1,256]{1,0:T(1,128)}, f32[1,256]{1,0:T(1,128)}, u32[]{:S(2)}, u32[]{:S(2)}) collective-permute-start(f32[1,256]{1,0:T(1,128)} %get-tuple-element.30.refs_0_), channel_id=1, source_target_pairs={{0,1},{1,0},{2,3},{3,2},{4,5},{5,4},{6,7},{7,6},{8,9},{9,8},{10,11... | collective-permute-start | bytes 3080 | tf_op jit(solution)/shard_map/ppermute | solution.py:426

commit v3 on v1

--- a/solution.py
+++ b/solution.py
@@ -40,6 +40,14 @@
         term = taps[offset : offset + 1] * scratch[pl.ds(start + 8 - offset, rows), :]
         total = term if total is None else total + term
     return total
+
+
+def split_conv(scratch, taps, start, rows):
+    reads = [scratch[pl.ds(start - offset, rows + 8), :] for offset in (0, 2, 4)]
+    odd = taps[1:2] * reads[0] + taps[3:4] * reads[1] + taps[5:6] * reads[2]
+    even = taps[0:1] * reads[0] + taps[2:3] * reads[1] + taps[4:5] * reads[2]
+    total = (even + pltpu.roll(odd, 1, 0))[8:]
+    return total + taps[6:7] * scratch[pl.ds(start + 8 - 6, rows), :]
 
 
 def tail_kernel(packed, q_ref, k_ref, v_ref, kb_ref, vb_ref, taps_ref, filt_ref, out_ref, ks, vs):
@@ -57,8 +65,8 @@
             key_taps = taps_ref[1, :, cols].astype(F32)
             value_taps = taps_ref[2, :, cols].astype(F32)
             for row in range(0, 128, 64):
-                key = short_conv(kt, key_taps, row + 8, 64)
-                value = short_conv(vt, value_taps, row + 8, 64)
+                key = split_conv(kt, key_taps, row + 8, 64)
+                value = split_conv(vt, value_taps, row + 8, 64)
                 out_ref[slot, row : row + 64, here] = (key * value).astype(BF16)
             last = [q_ref[:, cols].astype(F32)[8:], kt[136:144, :], vt[136:144, :]]
             if packed:

time: 65.3 us -> 65.5 us (level)
  no operation moved by 1% of the time
where the time goes in v3:
time: 65.5 us; the launch traced here: 64.8 us
  Pallas kernels  37.6 us (57%)
  starting transfers between devices  15.2 us (23%)
  waiting for transfers between devices  10.1 us (15%)
  local copies, waits for them, and re-layouts  1.28 us (2%)
  between operations  0.67 us (1%)
    all_to_all x2, starting transfers between devices, exchange(): lax.all_to_all(pieces, 'seq', split_axis=0, concat_axis=0, tiled=True)  11.5 us
    pallas_call x1, Pallas kernels, feature_call(): pl.pallas_call(feature_kernel, grid=(width // WIDE,), in_specs=[blocks[0]...  9.69 us
    pallas_call x3, Pallas kernels, norm_call(): pl.pallas_call(functools.partial(norm_kernel, channels, first_block, len(...  9.31 us
    pallas_call x1, Pallas kernels, main_call(): pl.pallas_call(functools.partial(main_kernel, group_size), grid_spec=pltp...  8.16 us
    all_to_all x2, waiting for transfers between devices, exchange(): lax.all_to_all(pieces, 'seq', split_axis=0, concat_axis=0, tiled=True)  7.94 us
    pallas_call x1, Pallas kernels, head_call(): pl.pallas_call(functools.partial(head_kernel, group_size), grid_spec=pltp...  5.11 us
    ppermute x6, starting transfers between devices, swap(): return lax.ppermute(array, axis, [(i, i ^ distance) for i in range(size)])  3.76 us
    pallas_call x1, Pallas kernels, tail_call(): pl.pallas_call(functools.partial(tail_kernel, packed), grid=(2,), in_spec...  3.26 us
  transfers between devices with their start and end apart: 8, of which 4 were waited for; matrix products, arithmetic and copies ran while one was open for 2% of the time, Pallas kernels for 37%

profile of v3, /device:TPU:0, one launch (start us, length us, event | category | flops | bytes accessed | tf_op | source)
XLA Modules:
  0.0 64.8 jit_solution(8091621902593122171)
XLA Ops:
  0.6 3.3 %tail.1 = bf16[8,160,256]{2,1,0:T(8,128)(2,1)} custom-call(bf16[512,2048]{1,0:T(8,128)(2,1)} %q_ref.5, bf16[512,2048]{1,0:T(8,128)(2,1)} %k_ref.5, bf16[512,2048]{1,0:T(8,128)(2,1)} %v_ref.5, bf16[512,2048]{1,0:T(8,128)(2,1)} %k_ref.5, bf16[512,2048]{1,0:T(8,128)(2,1)} %v_ref.5, bf16[3,7,2048]{2,1,0:T(8,128)(2,1)} %taps_ref.5, bf16[16,128]{1,0:T(8,128)(2,1)} %filt_ref.1), custom_call_target="tpu_custom_call" | custom-call | flops 7864320 | bytes 1572864 | tf_op jit(solution)/shard_map/tail/pallas_call | solution.py:85
  3.9 7.3 %all-to-all-start = ((bf16[8,160,256]{2,1,0:T(8,128)(2,1)}), bf16[8,160,256]{2,1,0:T(8,128)(2,1)}, u32[]{:S(2)}, u32[]{:S(2)}) async-start(bf16[8,160,256]{2,1,0:T(8,128)(2,1)} %tail.1), calls=%async_computation | async-start | bytes 1310720 | tf_op jit(solution)/shard_map/all_to_all | solution.py:438
  11.2 1.3 %reshape.7.refs_6_ = bf16[1,2048]{1,0:T(2,128)(2,1)} reshape(bf16[2048]{0:T(1024)(128)(2,1)} %param.15) | data formatting | bytes 8192 | tf_op jit(solution)/shard_map/reshape | solution.py:454
  12.5 9.7 %features.1 = (bf16[512,2048]{1,0:T(8,128)(2,1)}, f32[144,2048]{1,0:T(8,128)}, f32[384,2048]{1,0:T(8,128)}) custom-call(bf16[512,2048]{1,0:T(8,128)(2,1)} %q_ref.5, bf16[512,2048]{1,0:T(8,128)(2,1)} %k_ref.5, bf16[512,2048]{1,0:T(8,128)(2,1)} %v_ref.5, bf16[3,7,2048]{2,1,0:T(8,128)(2,1)} %taps_ref.5), custom_call_target="tpu_custom_call" | custom-call | flops 47185920 | bytes 13631488 | tf_op jit(solution)/shard_map/features/pallas_call | solution.py:135
  22.1 6.4 %all-to-all-done.in_ref.filt_ref = bf16[8,160,256]{2,1,0:T(8,128)(2,1)} async-done(((bf16[8,160,256]{2,1,0:T(8,128)(2,1)}), bf16[8,160,256]{2,1,0:T(8,128)(2,1)}, u32[]{:S(2)}, u32[]{:S(2)}) %all-to-all-start) | async-done | bytes 655392 | tf_op jit(solution)/shard_map/all_to_all | solution.py:438
  28.6 2.0 %route.1 = bf16[8,160,256]{2,1,0:T(8,128)(2,1)} custom-call(s32[8]{0:T(128)} %pred_ref.3, bf16[8,160,256]{2,1,0:T(8,128)(2,1)} %all-to-all-done.in_ref.filt_ref), custom_call_target="tpu_custom_call" | custom-call | bytes 1310720 | tf_op jit(solution)/shard_map/route/pallas_call | solution.py:156
  30.6 4.2 %all-to-all-start.1 = ((bf16[8,160,256]{2,1,0:T(8,128)(2,1)}), bf16[8,160,256]{2,1,0:T(8,128)(2,1)}, u32[]{:S(2)}, u32[]{:S(2)}) async-start(bf16[8,160,256]{2,1,0:T(8,128)(2,1)} %route.1), calls=%async_computation.1 | async-start | bytes 1310720 | tf_op jit(solution)/shard_map/all_to_all | solution.py:438
  34.8 8.2 %conv.1 = (bf16[512,2048]{1,0:T(8,128)(2,1)}, f32[1,384]{1,0:T(1,128)}, f32[128,256]{1,0:T(8,128)}) custom-call(s32[8]{0:T(128)} %len_ref.9, f32[384,2048]{1,0:T(8,128)} %get-tuple-element.20.query_ref, bf16[512,2048]{1,0:T(8,128)(2,1)} %get-tuple-element.21.u_ref, bf16[512,2048]{1,0:T(8,128)(2,1)} %refs_5_.5, bf16[8,160,256]{2,1,0:T(8,128)(2,1)} %all-to-all-done.in_ref.filt_ref), custom_call_target="tpu_custom_call" | custom-call | flops 4294967296 | bytes 12582912 | tf_op jit(solution)/shard_map/conv/pallas_call | solution.py:254
  43.0 0.3 collective-permute-start.2
  43.2 1.3 %collective-permute-start.1 = (f32[1,384]{1,0:T(1,128)}, f32[1,384]{1,0:T(1,128)}, u32[]{:S(2)}, u32[]{:S(2)}) collective-permute-start(f32[1,384]{1,0:T(1,128)} %get-tuple-element.23.refs_0_), channel_id=1, source_target_pairs={{0,2},{1,3},{2,0},{3,1},{4,6},{5,7},{6,4},{7,5},{8,10},{9,11},{10,... | collective-permute-start | bytes 4616 | tf_op jit(solution)/shard_map/ppermute | solution.py:434
  44.5 0.3 collective-permute-start
  44.8 1.5 %collective-permute-done.2.refs_3_ = f32[1,384]{1,0:T(1,128)} collective-permute-done((f32[1,384]{1,0:T(1,128)}, f32[1,384]{1,0:T(1,128)}, u32[]{:S(2)}, u32[]{:S(2)}) %collective-permute-start.2) | collective-permute-done | bytes 1568 | tf_op jit(solution)/shard_map/ppermute | solution.py:434
  46.3 0.7 %collective-permute-done.1.refs_2_ = f32[1,384]{1,0:T(1,128)} collective-permute-done((f32[1,384]{1,0:T(1,128)}, f32[1,384]{1,0:T(1,128)}, u32[]{:S(2)}, u32[]{:S(2)}) %collective-permute-start.1) | collective-permute-done | bytes 1568 | tf_op jit(solution)/shard_map/ppermute | solution.py:434
  47.0 3.3 %norm1.1.refs_7_ = bf16[512,2048]{1,0:T(8,128)(2,1)} custom-call(s32[8]{0:T(128)} %len_ref.9, f32[1,384]{1,0:T(1,128)} %get-tuple-element.23.refs_0_, f32[1,384]{1,0:T(1,128)} %collective-permute-done.refs_1_, f32[1,384]{1,0:T(1,128)} %collective-permute-done.1.refs_2_, f32[1,384]{1,0:T(1,128)} %collective-permute-done.2.refs_3_, ...), custom_call_target="tpu_custom_call" | custom-call | flops 3145728 | bytes 3145728 | tf_op jit(solution)/shard_map/norm1/pallas_call | solution.py:419
  50.3 1.5 %all-to-all-done.1.held = bf16[8,160,256]{2,1,0:T(8,128)(2,1)} async-done(((bf16[8,160,256]{2,1,0:T(8,128)(2,1)}), bf16[8,160,256]{2,1,0:T(8,128)(2,1)}, u32[]{:S(2)}, u32[]{:S(2)}) %all-to-all-start.1) | async-done | bytes 655392 | tf_op jit(solution)/shard_map/all_to_all | solution.py:438
  51.8 5.1 %head.1 = (bf16[512,2048]{1,0:T(8,128)(2,1)}, f32[1,256]{1,0:T(1,128)}) custom-call(s32[8]{0:T(128)} %pred_ref.3, s32[8]{0:T(128)} %len_ref.9, bf16[8,160,256]{2,1,0:T(8,128)(2,1)} %all-to-all-done.1.held, f32[144,2048]{1,0:T(8,128)} %get-tuple-element.27.query_ref, bf16[512,2048]{1,0:T(8,128)(2,1)} %q_ref.5, ...), custom_call_target="tpu_custom_call", output_to_operand_aliasing={{0}: (11, {})} | custom-call | flops 1073741824 | bytes 3145728 | tf_op jit(solution)/shard_map/head/pallas_call | solution.py:353
  56.9 0.1 collective-permute-start.5
  57.0 1.5 %collective-permute-start.4 = (f32[1,256]{1,0:T(1,128)}, f32[1,256]{1,0:T(1,128)}, u32[]{:S(2)}, u32[]{:S(2)}) collective-permute-start(f32[1,256]{1,0:T(1,128)} %get-tuple-element.30.refs_0_), channel_id=1, source_target_pairs={{0,2},{1,3},{2,0},{3,1},{4,6},{5,7},{6,4},{7,5},{8,10},{9,11},{10,... | collective-permute-start | bytes 3080 | tf_op jit(solution)/shard_map/ppermute | solution.py:434
  58.5 0.3 collective-permute-start.3
  58.9 3.0 %norm3.1.refs_7_ = bf16[512,2048]{1,0:T(8,128)(2,1)} custom-call(s32[8]{0:T(128)} %len_ref.9, f32[1,384]{1,0:T(1,128)} %get-tuple-element.23.refs_0_, f32[1,384]{1,0:T(1,128)} %collective-permute-done.refs_1_, f32[1,384]{1,0:T(1,128)} %collective-permute-done.1.refs_2_, f32[1,384]{1,0:T(1,128)} %collective-permute-done.2.refs_3_, ...), custom_call_target="tpu_custom_call", output_to_operand_aliasing={{}: (8, {})} | custom-call | flops 1572864 | bytes 1572864 | tf_op jit(solution)/shard_map/norm3/pallas_call | solution.py:419
  61.8 0.0 collective-permute-done.5.refs_3_
  61.8 0.0 collective-permute-done.4.refs_2_
  61.8 0.0 collective-permute-done.3.refs_1_
  61.8 3.0 %norm0.1 = bf16[512,2048]{1,0:T(8,128)(2,1)} custom-call(s32[8]{0:T(128)} %len_ref.9, f32[1,256]{1,0:T(1,128)} %get-tuple-element.30.refs_0_, f32[1,256]{1,0:T(1,128)} %collective-permute-done.3.refs_1_, f32[1,256]{1,0:T(1,128)} %collective-permute-done.4.refs_2_, f32[1,256]{1,0:T(1,128)} %collective-permute-done.5.refs_3_, ...), custom_call_target="tpu_custom_call", output_to_operand_aliasing={{}: (8, {})} | custom-call | flops 1769472 | bytes 1769472 | tf_op jit(solution)/shard_map/norm0/pallas_call | solution.py:419
  (1 shorter events, 0.0 us)
Async XLA Ops:
  3.9 24.7 %all-to-all-start = ((bf16[8,160,256]{2,1,0:T(8,128)(2,1)}), bf16[8,160,256]{2,1,0:T(8,128)(2,1)}, u32[]{:S(2)}, u32[]{:S(2)}) async-start(bf16[8,160,256]{2,1,0:T(8,128)(2,1)} %tail.1), calls=%async_computation | async-start | bytes 1310720 | tf_op jit(solution)/shard_map/all_to_all | solution.py:438
  30.6 21.2 %all-to-all-start.1 = ((bf16[8,160,256]{2,1,0:T(8,128)(2,1)}), bf16[8,160,256]{2,1,0:T(8,128)(2,1)}, u32[]{:S(2)}, u32[]{:S(2)}) async-start(bf16[8,160,256]{2,1,0:T(8,128)(2,1)} %route.1), calls=%async_computation.1 | async-start | bytes 1310720 | tf_op jit(solution)/shard_map/all_to_all | solution.py:438
  43.0 3.3 %collective-permute-start.2 = (f32[1,384]{1,0:T(1,128)}, f32[1,384]{1,0:T(1,128)}, u32[]{:S(2)}, u32[]{:S(2)}) collective-permute-start(f32[1,384]{1,0:T(1,128)} %get-tuple-element.23.refs_0_), channel_id=1, source_target_pairs={{0,3},{1,2},{2,1},{3,0},{4,7},{5,6},{6,5},{7,4},{8,11},{9,10},{10,... | collective-permute-start | bytes 4616 | tf_op jit(solution)/shard_map/ppermute | solution.py:434
  43.2 3.7 %collective-permute-start.1 = (f32[1,384]{1,0:T(1,128)}, f32[1,384]{1,0:T(1,128)}, u32[]{:S(2)}, u32[]{:S(2)}) collective-permute-start(f32[1,384]{1,0:T(1,128)} %get-tuple-element.23.refs_0_), channel_id=1, source_target_pairs={{0,2},{1,3},{2,0},{3,1},{4,6},{5,7},{6,4},{7,5},{8,10},{9,11},{10,... | collective-permute-start | bytes 4616 | tf_op jit(solution)/shard_map/ppermute | solution.py:434
  44.5 2.4 %collective-permute-start = (f32[1,384]{1,0:T(1,128)}, f32[1,384]{1,0:T(1,128)}, u32[]{:S(2)}, u32[]{:S(2)}) collective-permute-start(f32[1,384]{1,0:T(1,128)} %get-tuple-element.23.refs_0_), channel_id=1, source_target_pairs={{0,1},{1,0},{2,3},{3,2},{4,5},{5,4},{6,7},{7,6},{8,9},{9,8},{10,11... | collective-permute-start | bytes 4616 | tf_op jit(solution)/shard_map/ppermute | solution.py:434
  56.9 4.9 %collective-permute-start.5 = (f32[1,256]{1,0:T(1,128)}, f32[1,256]{1,0:T(1,128)}, u32[]{:S(2)}, u32[]{:S(2)}) collective-permute-start(f32[1,256]{1,0:T(1,128)} %get-tuple-element.30.refs_0_), channel_id=1, source_target_pairs={{0,3},{1,2},{2,1},{3,0},{4,7},{5,6},{6,5},{7,4},{8,11},{9,10},{10,... | collective-permute-start | bytes 3080 | tf_op jit(solution)/shard_map/ppermute | solution.py:434
  57.0 4.8 %collective-permute-start.4 = (f32[1,256]{1,0:T(1,128)}, f32[1,256]{1,0:T(1,128)}, u32[]{:S(2)}, u32[]{:S(2)}) collective-permute-start(f32[1,256]{1,0:T(1,128)} %get-tuple-element.30.refs_0_), channel_id=1, source_target_pairs={{0,2},{1,3},{2,0},{3,1},{4,6},{5,7},{6,4},{7,5},{8,10},{9,11},{10,... | collective-permute-start | bytes 3080 | tf_op jit(solution)/shard_map/ppermute | solution.py:434
  58.5 3.3 %collective-permute-start.3 = (f32[1,256]{1,0:T(1,128)}, f32[1,256]{1,0:T(1,128)}, u32[]{:S(2)}, u32[]{:S(2)}) collective-permute-start(f32[1,256]{1,0:T(1,128)} %get-tuple-element.30.refs_0_), channel_id=1, source_target_pairs={{0,1},{1,0},{2,3},{3,2},{4,5},{5,4},{6,7},{7,6},{8,9},{9,8},{10,11... | collective-permute-start | bytes 3080 | tf_op jit(solution)/shard_map/ppermute | solution.py:434

commit v4 on v1

--- a/solution.py
+++ b/solution.py
@@ -20,10 +20,6 @@
 PACKED = 160
 OPENING = 144
 VMEM_LIMIT = 64 * 1024 * 1024
-
-
-def unfold(picked):
-    return jnp.concatenate([picked[:, i * LANES : (i + 1) * LANES] for i in range(picked.shape[1] // LANES)])
 
 
 def params():
@@ -183,12 +179,16 @@
 
 
 def pick_groups(result, group_size, rows=BLOCK):
-    shape = (rows, result.shape[1])
-    group = (lax.broadcasted_iota(jnp.int32, shape, 1) & (LANES - 1)) // group_size
-    picked = result[:rows]
-    for g in range(1, LANES // group_size):
-        picked = jnp.where(group == g, result[g * rows : (g + 1) * rows], picked)
-    return picked
+    lane = lax.broadcasted_iota(jnp.int32, (rows, LANES), 1)
+    later = [lane >= g * group_size for g in range(LANES // group_size)]
+    blocks = []
+    for first in range(0, result.shape[1], LANES):
+        part = result[:, first : first + LANES]
+        picked = part[:rows]
+        for g in range(1, LANES // group_size):
+            picked = jnp.where(later[g], part[g * rows : (g + 1) * rows], picked)
+        blocks.append(picked)
+    return jnp.concatenate(blocks) if len(blocks) > 1 else blocks[0]
 
 
 def main_kernel(group_size, len_ref, query_ref, u_ref, res_ref, filt_ref, mixed_ref, sum_ref, lines_ref, acc):
@@ -219,7 +219,7 @@
                         windows.append(u_ref[low : first + BLOCK, cols])
                 result = jnp.dot(matrix, jnp.concatenate(windows, axis=1), preferred_element_type=F32)
                 picked = pick_groups(result, group_size)
-                filtered = unfold(picked)
+                filtered = picked
                 here = slice(start - 128, start - 128 + SIDE * BLOCK)
                 row = lax.broadcasted_iota(jnp.int32, filtered.shape, 0) + start
                 mixed = jnp.where(row < length, query_ref[here, cols] * filtered, 0.0).astype(BF16)
@@ -315,7 +315,7 @@
                 windows = [extended[low : low + WINDOW] for low in lows]
                 result = jnp.dot(matrix, jnp.concatenate(windows, axis=1), preferred_element_type=F32)
                 picked = pick_groups(result, group_size)
-                parts.append((first, SIDE * BLOCK, unfold(picked)))
+                parts.append((first, SIDE * BLOCK, picked))
             edge = OPENING - 128
             edge_matrix = jnp.concatenate([matrix[g * BLOCK : g * BLOCK + edge] for g in range(per_lane)])
             edge_result = jnp.dot(edge_matrix, extended[128 : 128 + WINDOW], preferred_element_type=F32)

time: 65.3 us -> 65.3 us (level)
  no operation moved by 1% of the time
where the time goes in v4:
time: 65.3 us; the launch traced here: 64.7 us
  Pallas kernels  37.4 us (57%)
  starting transfers between devices  15.2 us (23%)
  waiting for transfers between devices  10.1 us (15%)
  local copies, waits for them, and re-layouts  1.28 us (2%)
  between operations  0.67 us (1%)
    all_to_all x2, starting transfers between devices, exchange(): lax.all_to_all(pieces, 'seq', split_axis=0, concat_axis=0, tiled=True)  11.5 us
    pallas_call x1, Pallas kernels, feature_call(): pl.pallas_call(feature_kernel, grid=(width // WIDE,), in_specs=[blocks[0]...  9.69 us
    pallas_call x3, Pallas kernels, norm_call(): pl.pallas_call(functools.partial(norm_kernel, channels, first_block, len(...  9.31 us
    pallas_call x1, Pallas kernels, main_call(): pl.pallas_call(functools.partial(main_kernel, group_size), grid_spec=pltp...  8.14 us
    all_to_all x2, waiting for transfers between devices, exchange(): lax.all_to_all(pieces, 'seq', split_axis=0, concat_axis=0, tiled=True)  7.95 us
    pallas_call x1, Pallas kernels, head_call(): pl.pallas_call(functools.partial(head_kernel, group_size), grid_spec=pltp...  5.09 us
    ppermute x6, starting transfers between devices, swap(): return lax.ppermute(array, axis, [(i, i ^ distance) for i in range(size)])  3.76 us
    pallas_call x1, Pallas kernels, tail_call(): pl.pallas_call(functools.partial(tail_kernel, packed), grid=(2,), in_spec...  3.11 us
  transfers between devices with their start and end apart: 8, of which 4 were waited for; matrix products, arithmetic and copies ran while one was open for 2% of the time, Pallas kernels for 37%

profile of v4, /device:TPU:0, one launch (start us, length us, event | category | flops | bytes accessed | tf_op | source)
XLA Modules:
  0.0 64.7 jit_solution(16870356124981668434)
XLA Ops:
  0.6 3.1 %tail.1 = bf16[8,160,256]{2,1,0:T(8,128)(2,1)} custom-call(bf16[512,2048]{1,0:T(8,128)(2,1)} %q_ref.5, bf16[512,2048]{1,0:T(8,128)(2,1)} %k_ref.5, bf16[512,2048]{1,0:T(8,128)(2,1)} %v_ref.5, bf16[512,2048]{1,0:T(8,128)(2,1)} %k_ref.5, bf16[512,2048]{1,0:T(8,128)(2,1)} %v_ref.5, bf16[3,7,2048]{2,1,0:T(8,128)(2,1)} %taps_ref.5, bf16[16,128]{1,0:T(8,128)(2,1)} %filt_ref.1), custom_call_target="tpu_custom_call" | custom-call | flops 7864320 | bytes 1572864 | tf_op jit(solution)/shard_map/tail/pallas_call | solution.py:73
  3.7 7.3 %all-to-all-start = ((bf16[8,160,256]{2,1,0:T(8,128)(2,1)}), bf16[8,160,256]{2,1,0:T(8,128)(2,1)}, u32[]{:S(2)}, u32[]{:S(2)}) async-start(bf16[8,160,256]{2,1,0:T(8,128)(2,1)} %tail.1), calls=%async_computation | async-start | bytes 1310720 | tf_op jit(solution)/shard_map/all_to_all | solution.py:430
  11.0 1.3 %reshape.7.refs_6_ = bf16[1,2048]{1,0:T(2,128)(2,1)} reshape(bf16[2048]{0:T(1024)(128)(2,1)} %param.15) | data formatting | bytes 8192 | tf_op jit(solution)/shard_map/reshape | solution.py:446
  12.3 9.7 %features.1 = (bf16[512,2048]{1,0:T(8,128)(2,1)}, f32[144,2048]{1,0:T(8,128)}, f32[384,2048]{1,0:T(8,128)}) custom-call(bf16[512,2048]{1,0:T(8,128)(2,1)} %q_ref.5, bf16[512,2048]{1,0:T(8,128)(2,1)} %k_ref.5, bf16[512,2048]{1,0:T(8,128)(2,1)} %v_ref.5, bf16[3,7,2048]{2,1,0:T(8,128)(2,1)} %taps_ref.5), custom_call_target="tpu_custom_call" | custom-call | flops 47185920 | bytes 13631488 | tf_op jit(solution)/shard_map/features/pallas_call | solution.py:123
  22.0 6.4 %all-to-all-done.in_ref.filt_ref = bf16[8,160,256]{2,1,0:T(8,128)(2,1)} async-done(((bf16[8,160,256]{2,1,0:T(8,128)(2,1)}), bf16[8,160,256]{2,1,0:T(8,128)(2,1)}, u32[]{:S(2)}, u32[]{:S(2)}) %all-to-all-start) | async-done | bytes 655392 | tf_op jit(solution)/shard_map/all_to_all | solution.py:430
  28.4 2.0 %route.1 = bf16[8,160,256]{2,1,0:T(8,128)(2,1)} custom-call(s32[8]{0:T(128)} %pred_ref.3, bf16[8,160,256]{2,1,0:T(8,128)(2,1)} %all-to-all-done.in_ref.filt_ref), custom_call_target="tpu_custom_call" | custom-call | bytes 1310720 | tf_op jit(solution)/shard_map/route/pallas_call | solution.py:144
  30.5 4.2 %all-to-all-start.1 = ((bf16[8,160,256]{2,1,0:T(8,128)(2,1)}), bf16[8,160,256]{2,1,0:T(8,128)(2,1)}, u32[]{:S(2)}, u32[]{:S(2)}) async-start(bf16[8,160,256]{2,1,0:T(8,128)(2,1)} %route.1), calls=%async_computation.1 | async-start | bytes 1310720 | tf_op jit(solution)/shard_map/all_to_all | solution.py:430
  34.7 8.1 %conv.1 = (bf16[512,2048]{1,0:T(8,128)(2,1)}, f32[1,384]{1,0:T(1,128)}, f32[128,256]{1,0:T(8,128)}) custom-call(s32[8]{0:T(128)} %len_ref.9, f32[384,2048]{1,0:T(8,128)} %get-tuple-element.20.query_ref, bf16[512,2048]{1,0:T(8,128)(2,1)} %get-tuple-element.21.u_ref, bf16[512,2048]{1,0:T(8,128)(2,1)} %refs_5_.5, bf16[8,160,256]{2,1,0:T(8,128)(2,1)} %all-to-all-done.in_ref.filt_ref), custom_call_target="tpu_custom_call" | custom-call | flops 4294967296 | bytes 12582912 | tf_op jit(solution)/shard_map/conv/pallas_call | solution.py:246
  42.8 0.3 collective-permute-start.2
  43.1 1.3 %collective-permute-start.1 = (f32[1,384]{1,0:T(1,128)}, f32[1,384]{1,0:T(1,128)}, u32[]{:S(2)}, u32[]{:S(2)}) collective-permute-start(f32[1,384]{1,0:T(1,128)} %get-tuple-element.23.refs_0_), channel_id=1, source_target_pairs={{0,2},{1,3},{2,0},{3,1},{4,6},{5,7},{6,4},{7,5},{8,10},{9,11},{10,... | collective-permute-start | bytes 4616 | tf_op jit(solution)/shard_map/ppermute | solution.py:426
  44.4 0.3 collective-permute-start
  44.7 1.5 %collective-permute-done.2.refs_3_ = f32[1,384]{1,0:T(1,128)} collective-permute-done((f32[1,384]{1,0:T(1,128)}, f32[1,384]{1,0:T(1,128)}, u32[]{:S(2)}, u32[]{:S(2)}) %collective-permute-start.2) | collective-permute-done | bytes 1568 | tf_op jit(solution)/shard_map/ppermute | solution.py:426
  46.1 0.7 %collective-permute-done.1.refs_2_ = f32[1,384]{1,0:T(1,128)} collective-permute-done((f32[1,384]{1,0:T(1,128)}, f32[1,384]{1,0:T(1,128)}, u32[]{:S(2)}, u32[]{:S(2)}) %collective-permute-start.1) | collective-permute-done | bytes 1568 | tf_op jit(solution)/shard_map/ppermute | solution.py:426
  46.8 0.0 collective-permute-done.refs_1_
  46.8 3.3 %norm1.1.refs_7_ = bf16[512,2048]{1,0:T(8,128)(2,1)} custom-call(s32[8]{0:T(128)} %len_ref.9, f32[1,384]{1,0:T(1,128)} %get-tuple-element.23.refs_0_, f32[1,384]{1,0:T(1,128)} %collective-permute-done.refs_1_, f32[1,384]{1,0:T(1,128)} %collective-permute-done.1.refs_2_, f32[1,384]{1,0:T(1,128)} %collective-permute-done.2.refs_3_, ...), custom_call_target="tpu_custom_call" | custom-call | flops 3145728 | bytes 3145728 | tf_op jit(solution)/shard_map/norm1/pallas_call | solution.py:411
  50.2 1.5 %all-to-all-done.1.held = bf16[8,160,256]{2,1,0:T(8,128)(2,1)} async-done(((bf16[8,160,256]{2,1,0:T(8,128)(2,1)}), bf16[8,160,256]{2,1,0:T(8,128)(2,1)}, u32[]{:S(2)}, u32[]{:S(2)}) %all-to-all-start.1) | async-done | bytes 655392 | tf_op jit(solution)/shard_map/all_to_all | solution.py:430
  51.7 5.1 %head.1 = (bf16[512,2048]{1,0:T(8,128)(2,1)}, f32[1,256]{1,0:T(1,128)}) custom-call(s32[8]{0:T(128)} %pred_ref.3, s32[8]{0:T(128)} %len_ref.9, bf16[8,160,256]{2,1,0:T(8,128)(2,1)} %all-to-all-done.1.held, f32[144,2048]{1,0:T(8,128)} %get-tuple-element.27.query_ref, bf16[512,2048]{1,0:T(8,128)(2,1)} %q_ref.5, ...), custom_call_target="tpu_custom_call", output_to_operand_aliasing={{0}: (11, {})} | custom-call | flops 1073741824 | bytes 3145728 | tf_op jit(solution)/shard_map/head/pallas_call | solution.py:345
  56.8 0.1 collective-permute-start.5
  56.8 1.6 %collective-permute-start.4 = (f32[1,256]{1,0:T(1,128)}, f32[1,256]{1,0:T(1,128)}, u32[]{:S(2)}, u32[]{:S(2)}) collective-permute-start(f32[1,256]{1,0:T(1,128)} %get-tuple-element.30.refs_0_), channel_id=1, source_target_pairs={{0,2},{1,3},{2,0},{3,1},{4,6},{5,7},{6,4},{7,5},{8,10},{9,11},{10,... | collective-permute-start | bytes 3080 | tf_op jit(solution)/shard_map/ppermute | solution.py:426
  58.4 0.3 collective-permute-start.3
  58.7 3.0 %norm3.1.refs_7_ = bf16[512,2048]{1,0:T(8,128)(2,1)} custom-call(s32[8]{0:T(128)} %len_ref.9, f32[1,384]{1,0:T(1,128)} %get-tuple-element.23.refs_0_, f32[1,384]{1,0:T(1,128)} %collective-permute-done.refs_1_, f32[1,384]{1,0:T(1,128)} %collective-permute-done.1.refs_2_, f32[1,384]{1,0:T(1,128)} %collective-permute-done.2.refs_3_, ...), custom_call_target="tpu_custom_call", output_to_operand_aliasing={{}: (8, {})} | custom-call | flops 1572864 | bytes 1572864 | tf_op jit(solution)/shard_map/norm3/pallas_call | solution.py:411
  61.6 0.0 collective-permute-done.5.refs_3_
  61.7 0.0 collective-permute-done.3.refs_1_
  61.7 3.0 %norm0.1 = bf16[512,2048]{1,0:T(8,128)(2,1)} custom-call(s32[8]{0:T(128)} %len_ref.9, f32[1,256]{1,0:T(1,128)} %get-tuple-element.30.refs_0_, f32[1,256]{1,0:T(1,128)} %collective-permute-done.3.refs_1_, f32[1,256]{1,0:T(1,128)} %collective-permute-done.4.refs_2_, f32[1,256]{1,0:T(1,128)} %collective-permute-done.5.refs_3_, ...), custom_call_target="tpu_custom_call", output_to_operand_aliasing={{}: (8, {})} | custom-call | flops 1769472 | bytes 1769472 | tf_op jit(solution)/shard_map/norm0/pallas_call | solution.py:411
  (1 shorter events, 0.0 us)
Async XLA Ops:
  3.7 24.7 %all-to-all-start = ((bf16[8,160,256]{2,1,0:T(8,128)(2,1)}), bf16[8,160,256]{2,1,0:T(8,128)(2,1)}, u32[]{:S(2)}, u32[]{:S(2)}) async-start(bf16[8,160,256]{2,1,0:T(8,128)(2,1)} %tail.1), calls=%async_computation | async-start | bytes 1310720 | tf_op jit(solution)/shard_map/all_to_all | solution.py:430
  30.5 21.2 %all-to-all-start.1 = ((bf16[8,160,256]{2,1,0:T(8,128)(2,1)}), bf16[8,160,256]{2,1,0:T(8,128)(2,1)}, u32[]{:S(2)}, u32[]{:S(2)}) async-start(bf16[8,160,256]{2,1,0:T(8,128)(2,1)} %route.1), calls=%async_computation.1 | async-start | bytes 1310720 | tf_op jit(solution)/shard_map/all_to_all | solution.py:430
  42.8 3.3 %collective-permute-start.2 = (f32[1,384]{1,0:T(1,128)}, f32[1,384]{1,0:T(1,128)}, u32[]{:S(2)}, u32[]{:S(2)}) collective-permute-start(f32[1,384]{1,0:T(1,128)} %get-tuple-element.23.refs_0_), channel_id=1, source_target_pairs={{0,3},{1,2},{2,1},{3,0},{4,7},{5,6},{6,5},{7,4},{8,11},{9,10},{10,... | collective-permute-start | bytes 4616 | tf_op jit(solution)/shard_map/ppermute | solution.py:426
  43.1 3.7 %collective-permute-start.1 = (f32[1,384]{1,0:T(1,128)}, f32[1,384]{1,0:T(1,128)}, u32[]{:S(2)}, u32[]{:S(2)}) collective-permute-start(f32[1,384]{1,0:T(1,128)} %get-tuple-element.23.refs_0_), channel_id=1, source_target_pairs={{0,2},{1,3},{2,0},{3,1},{4,6},{5,7},{6,4},{7,5},{8,10},{9,11},{10,... | collective-permute-start | bytes 4616 | tf_op jit(solution)/shard_map/ppermute | solution.py:426
  44.4 2.4 %collective-permute-start = (f32[1,384]{1,0:T(1,128)}, f32[1,384]{1,0:T(1,128)}, u32[]{:S(2)}, u32[]{:S(2)}) collective-permute-start(f32[1,384]{1,0:T(1,128)} %get-tuple-element.23.refs_0_), channel_id=1, source_target_pairs={{0,1},{1,0},{2,3},{3,2},{4,5},{5,4},{6,7},{7,6},{8,9},{9,8},{10,11... | collective-permute-start | bytes 4616 | tf_op jit(solution)/shard_map/ppermute | solution.py:426
  56.8 4.9 %collective-permute-start.5 = (f32[1,256]{1,0:T(1,128)}, f32[1,256]{1,0:T(1,128)}, u32[]{:S(2)}, u32[]{:S(2)}) collective-permute-start(f32[1,256]{1,0:T(1,128)} %get-tuple-element.30.refs_0_), channel_id=1, source_target_pairs={{0,3},{1,2},{2,1},{3,0},{4,7},{5,6},{6,5},{7,4},{8,11},{9,10},{10,... | collective-permute-start | bytes 3080 | tf_op jit(solution)/shard_map/ppermute | solution.py:426
  56.8 4.8 %collective-permute-start.4 = (f32[1,256]{1,0:T(1,128)}, f32[1,256]{1,0:T(1,128)}, u32[]{:S(2)}, u32[]{:S(2)}) collective-permute-start(f32[1,256]{1,0:T(1,128)} %get-tuple-element.30.refs_0_), channel_id=1, source_target_pairs={{0,2},{1,3},{2,0},{3,1},{4,6},{5,7},{6,4},{7,5},{8,10},{9,11},{10,... | collective-permute-start | bytes 3080 | tf_op jit(solution)/shard_map/ppermute | solution.py:426
  58.4 3.3 %collective-permute-start.3 = (f32[1,256]{1,0:T(1,128)}, f32[1,256]{1,0:T(1,128)}, u32[]{:S(2)}, u32[]{:S(2)}) collective-permute-start(f32[1,256]{1,0:T(1,128)} %get-tuple-element.30.refs_0_), channel_id=1, source_target_pairs={{0,1},{1,0},{2,3},{3,2},{4,5},{5,4},{6,7},{7,6},{8,9},{9,8},{10,11... | collective-permute-start | bytes 3080 | tf_op jit(solution)/shard_map/ppermute | solution.py:426
